TPU v7x, 128 devices: a whole 4x4x4 slice. The times are simulated.
128 devices in a mesh: dp: 16 (over y, z), ctx: 8 (over x, core).
Axes of the slice: x: 4, y: 4, z: 4, core: 2. Of those that a mesh axis runs over, the one named last changes fastest.
Arguments:
- tokens: bfloat16 [32, 8192, 1280], P('dp', 'ctx'), may hold values from -16.77051 to 16.77051
- slot_param: bfloat16 [1280, 64], replicated, may hold values from -1 to 1
- w_in: bfloat16 [64, 1280, 5120], P('dp', None, 'ctx'), may hold values from -6 to 6
- w_out: bfloat16 [64, 5120, 1280], P('dp', 'ctx'), may hold values from -0.3125 to 0.3125
Outputs:
- mixed: bfloat16 [32, 8192, 1280], P('dp', 'ctx')
All inputs are finite; a program needn't handle non-finite values.
Results may differ from a plain program's by a relative error of at most 0.013.
Values may be sent and summed in bfloat16 or wider, within the bound.
No kernel may reach another device: no remote copies, remote signals or barrier semaphores. Data moves between devices by JAX's collectives and lax.ppermute only.
A program may use at most 64 MiB of HBM per device.

v0:
```python
import jax
import jax.numpy as jnp
from jax import lax
from jax.sharding import PartitionSpec as P


def on_device(tokens, slot_param, w_in, w_out):
    logits = jnp.einsum("ds,cnd->csn", slot_param, tokens, preferred_element_type=jnp.float32)
    local_top = jnp.max(logits, axis=2)
    peak = lax.pmax(local_top, "ctx")
    expd = jnp.exp(logits - peak[:, :, None])
    local_total = jnp.sum(expd, axis=2)
    dispatch = expd.astype(jnp.bfloat16)
    partial_value = jnp.einsum("csn,cnd->csd", dispatch, tokens, preferred_element_type=jnp.float32)
    row_top = jnp.max(logits, axis=1, keepdims=True)
    row_exp = jnp.exp(logits - row_top)
    combine = (row_exp / jnp.sum(row_exp, axis=1, keepdims=True)).astype(jnp.bfloat16)
    total, whole = lax.psum((local_total, partial_value), "ctx")
    slot_in = (whole / total[:, :, None]).astype(jnp.bfloat16)
    routed = lax.all_to_all(slot_in, "dp", split_axis=1, concat_axis=0, tiled=True)
    pre = jnp.einsum("bed,edf->bef", routed, w_in, preferred_element_type=jnp.float32)
    hidden = jax.nn.gelu(pre, approximate=False).astype(jnp.bfloat16)
    partial_out = jnp.einsum("bef,efd->bed", hidden, w_out, preferred_element_type=jnp.float32)
    returned = lax.all_to_all(partial_out, "dp", split_axis=0, concat_axis=1, tiled=True)
    expert_out = lax.psum(returned, "ctx").astype(jnp.bfloat16)
    mixed = jnp.einsum(
        "csn,csd->cnd", combine, expert_out, preferred_element_type=jnp.float32
    ).astype(jnp.bfloat16)
    return mixed


def solution(mesh):
    placed = (P("dp", "ctx", None), P(), P("dp", None, "ctx"), P("dp", "ctx", None))
    return jax.shard_map(
        on_device, mesh=mesh, in_specs=placed, out_specs=P("dp", "ctx", None), check_vma=False
    )
```

profile of v0, /device:TPU:1, one launch (start us, length us, event | category | flops | bytes accessed | tf_op | source)
XLA Modules:
  0.0 172.2 jit_solution(4182809617162183483)
XLA Ops:
  6.5 0.0 copy-start
  6.5 0.0 all-reduce.3.cloned.1.call-start
  6.5 0.9 copy-done
  7.5 4.3 %fusion.91 = (f32[2,64]{1,0:T(2,128)S(1)}, f32[2,64,1024]{2,1,0:T(8,128)S(1)}) fusion(bf16[2,1024,1280]{2,1,0:T(8,128)(2,1)} %param.4, bf16[1280,64]{0,1:T(8,128)(2,1)S(1)} %copy-done), kind=kOutput, calls=%fused_computation.103 | convolution fusion | flops 335675264 | bytes 5931520 | tf_op jit(solution)/shard_map/ds,cnd->csn/dot_general | solution.py:8
  11.7 13.2 %pmax.7 = f32[2,64]{1,0:T(2,128)S(1)} all-reduce(f32[2,64]{1,0:T(2,128)S(1)} %get-tuple-element.5), channel_id=1, replica_groups=mesh['dp'=16,'ctx'=8] {'ctx'}, use_global_device_ids=true, to_apply=%region_3.0 | all-reduce | flops 128 | bytes 1024 | tf_op jit(solution)/shard_map/pmax | solution.py:10
  24.9 4.4 %fusion.24 = f32[2,64,1280]{2,1,0:T(8,128)} fusion(bf16[2,1024,1280]{2,1,0:T(8,128)(2,1)} %param.4, f32[2,64,1024]{2,1,0:T(8,128)S(1)} %get-tuple-element.6, f32[2,64]{1,0:T(2,128)S(1)} %pmax.7), kind=kOutput, calls=%fused_computation.38 | convolution fusion | flops 335806464 | bytes 6423040 | tf_op jit(solution)/shard_map/csn,cnd->csd/dot_general | solution.py:14
  29.3 0.0 all-reduce.3.cloned.1.call-update
  29.3 0.2 fusion.3
  29.5 14.7 %psum.22 = f32[2,64]{1,0:T(2,128)S(1)} all-reduce(f32[2,64]{1,0:T(2,128)S(1)} %fusion.3), channel_id=1, replica_groups=mesh['dp'=16,'ctx'=8] {'ctx'}, use_global_device_ids=true, to_apply=%region_6.0 | all-reduce | flops 128 | bytes 1024 | tf_op jit(solution)/shard_map/psum | solution.py:18
  44.2 46.6 %all-reduce.3.cloned.1.call-done = f32[2,64,1280]{2,1,0:T(8,128)} async-done(((f32[2,64,1280]{2,1,0:T(8,128)}), f32[2,64,1280]{2,1,0:T(8,128)}) %all-reduce.3.cloned.1.call-update) | async-done | bytes 655376 | tf_op jit(solution)/shard_map/psum | solution.py:18
  90.8 1.2 divide_convert_fusion
  92.0 0.3 copy.7
  92.3 14.3 %all_to_all.36 = bf16[2,64,1280]{2,0,1:T(2,128)(2,1)S(1)} all-to-all(bf16[2,64,1280]{2,0,1:T(2,128)(2,1)S(1)} %copy.7), channel_id=1, replica_groups=mesh['dp'=16,'ctx'=8] {'dp'}, dimensions={1} | all-to-all | bytes 655360 | tf_op jit(solution)/shard_map/all_to_all | solution.py:20
  106.6 0.2 copy.14
  106.8 0.1 all_to_all.29
  107.0 7.4 %convolution_bitcast_fusion = f32[32,4,1280]{2,0,1:T(8,128)S(1)} fusion(bf16[4,640,1280]{2,1,0:T(8,128)(2,1)} %param.7, bf16[32,4,1280]{2,0,1:T(8,128)(2,1)S(1)} %all_to_all.29, bf16[4,1280,640]{2,1,0:T(8,128)(2,1)} %param.6), kind=kOutput, calls=%fused_computation.2 | convolution fusion | flops 424755200 | bytes 14090240 | tf_op jit(solution)/shard_map/bef,efd->bed/dot_general | solution.py:23
  114.3 1.3 copy.9
  115.6 3.6 %all-to-all-start.1 = ((f32[32,4,1280]{2,1,0:T(4,128)}), f32[32,4,1280]{2,1,0:T(4,128)S(1)}, u32[]{:S(2)}, u32[]{:S(2)}) async-start(f32[32,4,1280]{2,1,0:T(4,128)} %copy.9), calls=%async_computation.1 | async-start | bytes 1310720 | tf_op jit(solution)/shard_map/all_to_all | solution.py:24
  119.2 0.1 fusion.92
  119.4 9.6 %all-to-all-done.1 = f32[32,4,1280]{2,1,0:T(4,128)S(1)} async-done(((f32[32,4,1280]{2,1,0:T(4,128)}), f32[32,4,1280]{2,1,0:T(4,128)S(1)}, u32[]{:S(2)}, u32[]{:S(2)}) %all-to-all-start.1) | async-done | bytes 655392 | tf_op jit(solution)/shard_map/all_to_all | solution.py:24
  129.0 0.2 all_to_all.33
  129.2 32.1 %all-reduce.4 = bf16[2,64,1280]{2,1,0:T(8,128)(2,1)S(1)} all-reduce(f32[2,64,1280]{2,1,0:T(8,128)S(1)} %all_to_all.33), channel_id=1, replica_groups=mesh['dp'=16,'ctx'=8] {'ctx'}, use_global_device_ids=true, to_apply=%region_7.0 | all-reduce | flops 163840 | bytes 983040 | tf_op jit(solution)/shard_map/psum | solution.py:25
  161.4 4.0 %convolution_convert_fusion = bf16[2,1024,1280]{2,1,0:T(8,128)(2,1)} fusion(bf16[2,64,1280]{2,1,0:T(8,128)(2,1)S(1)} %all-reduce.4, f32[2,1024]{1,0:T(2,128)S(1)} %fusion.92, f32[2,64,1024]{2,1,0:T(8,128)S(1)} %get-tuple-element.6), kind=kOutput, calls=%fused_computation.1 | convolution fusion | flops 338561088 | bytes 6103040 | tf_op jit(solution)/shard_map/csn,csd->cnd/dot_general | solution.py:26
  (1 shorter events, 0.0 us)
Async XLA Ops:
  6.5 0.9 copy-start
  6.5 84.2 %all-reduce.3.cloned.1.call-start = ((), (), s32[]{:S(2)}) async-start(), calls=%async_computation.2 | async-start | bytes 1310720 | tf_op jit(solution)/shard_map/psum | solution.py:18
  115.6 13.3 %all-to-all-start.1 = ((f32[32,4,1280]{2,1,0:T(4,128)}), f32[32,4,1280]{2,1,0:T(4,128)S(1)}, u32[]{:S(2)}, u32[]{:S(2)}) async-start(f32[32,4,1280]{2,1,0:T(4,128)} %copy.9), calls=%async_computation.1 | async-start | bytes 1310720 | tf_op jit(solution)/shard_map/all_to_all | solution.py:24
Sparse Core Ops, SparseCore 0:
  29.4 61.2 all-reduce.2
where the time goes:
time: 175 us; the launch traced here: 172 us
  blocking collectives  74.3 us (42%)
  waiting for transfers between devices  56.2 us (32%)
  matrix products  20 us (11%)
  between operations  13.4 us (8%)
  starting transfers between devices  3.6 us (2%)
  local copies, waits for them, and re-layouts  3.14 us (2%)
    psum x1, waiting for transfers between devices, on_device(): total, whole = lax.psum((local_total, partial_value), 'ctx')  46.6 us
    psum x1, blocking collectives, on_device(): expert_out = lax.psum(returned, 'ctx').astype(jnp.bfloat16)  32.1 us
    psum x1, blocking collectives, on_device(): total, whole = lax.psum((local_total, partial_value), 'ctx')  14.7 us
    all_to_all x1, blocking collectives, on_device(): lax.all_to_all(slot_in, 'dp', split_axis=1, concat_axis=0, tiled=True)  14.3 us
    pmax x1, blocking collectives, on_device(): peak = lax.pmax(local_top, 'ctx')  13.2 us
    all_to_all x1, waiting for transfers between devices, on_device(): lax.all_to_all(partial_out, 'dp', split_axis=0, concat_axis=1, tiled=True)  9.6 us
    dot_general x1, matrix products, on_device(): jnp.einsum('bef,efd->bed', hidden, w_out, preferred_element_type=jnp.floa...  7.38 us
    dot_general x1, matrix products, on_device(): jnp.einsum('csn,cnd->csd', dispatch, tokens, preferred_element_type=jnp.f...  4.4 us
  transfers between devices with their start and end apart: 2, of which 2 were waited for; matrix products, arithmetic and copies ran while one was open for 0% of the time, Pallas kernels for 0%

commit v1 on v0

v1 whole, which is shorter than its diff:
```python
import functools

import jax
import jax.numpy as jnp
import numpy as np
from jax import lax
from jax.experimental import pallas as pl
from jax.experimental.pallas import tpu as pltpu
from jax.sharding import PartitionSpec as P

F32 = jnp.float32
BF16 = jnp.bfloat16
HALF = 640
WIDE = HALF + 128
NT = (((1,), (1,)), ((), ()))


def with_stats(values, peak, high, low):
    lane = lax.broadcasted_iota(jnp.int32, (values.shape[0], 128), 1)
    stats = jnp.where(lane == 0, peak, jnp.where(lane == 1, high, jnp.where(lane == 2, low, 0.0)))
    return jnp.concatenate([values, stats], axis=1)


def split_total(total):
    high = total.astype(BF16).astype(F32)
    return high, total - high


def gather_kernel(pieces, tokens_hbm, slots_ref, send_ref, keep_ref, logits_ref, tokens, whole, sems):
    core = lax.axis_index("core")
    mine = pl.ds(pl.multiple_of(core * HALF, 128), HALF)
    other = pl.ds(pl.multiple_of((1 - core) * HALF, 128), HALF)
    clips, count, _ = tokens.shape
    step = count // pieces

    def copy(b, i):
        rows = pl.ds(i * step, step)
        return pltpu.make_async_copy(tokens_hbm.at[b, rows], tokens.at[b, rows], sems.at[b, i])

    for b in range(clips):
        for i in range(pieces):
            copy(b, i).start()
    for b in range(clips):
        for i in range(pieces):
            copy(b, i).wait()
            logits_ref[b, :, pl.ds(i * step, step)] = lax.dot_general(
                slots_ref[...], tokens[b, pl.ds(i * step, step), :], NT, preferred_element_type=F32
            )
        logits = logits_ref[b]
        peak = jnp.max(logits, axis=1, keepdims=True).astype(BF16).astype(F32)
        expd = jnp.exp(logits - peak)
        total = jnp.sum(expd, axis=1, keepdims=True)
        whole[...] = jnp.dot(expd.astype(BF16), tokens[b], preferred_element_type=F32)
        high, low = split_total(total)
        send_ref[b] = with_stats(whole[:, other], peak, high, low).astype(BF16)
        keep_ref[b] = with_stats(whole[:, mine], peak, total, jnp.zeros_like(total))


def gather(tokens, slots_t):
    clips, count, width = tokens.shape
    slots = slots_t.shape[0]
    pieces = 4
    return pl.pallas_call(
        functools.partial(gather_kernel, pieces),
        out_shape=[
            jax.ShapeDtypeStruct((clips, slots, WIDE), BF16),
            jax.ShapeDtypeStruct((clips, slots, WIDE), F32),
            jax.ShapeDtypeStruct((clips, slots, count), F32),
        ],
        in_specs=[pl.BlockSpec(memory_space=pl.ANY), pl.BlockSpec(memory_space=pltpu.VMEM)],
        out_specs=[pl.BlockSpec(memory_space=pltpu.VMEM)] * 3,
        scratch_shapes=[
            pltpu.VMEM((clips, count, width), BF16),
            pltpu.VMEM((slots, width), F32),
            pltpu.SemaphoreType.DMA((clips, pieces)),
        ],
        compiler_params=pltpu.CompilerParams(vmem_limit_bytes=40 << 20),
        cost_estimate=pl.CostEstimate(
            flops=4 * clips * slots * count * width,
            bytes_accessed=2 * clips * count * width,
            transcendentals=clips * slots * count,
        ),
        name="gather",
    )(tokens, slots_t)


def pack_kernel(keep_ref, recv_ref, out_ref):
    halves = []
    for b in range(2):
        kept, got = keep_ref[b], recv_ref[b].astype(F32)
        peak_k, peak_g = kept[:, HALF : HALF + 1], got[:, HALF : HALF + 1]
        peak = jnp.maximum(peak_k, peak_g)
        scale_k, scale_g = jnp.exp(peak_k - peak), jnp.exp(peak_g - peak)
        total = scale_k * kept[:, HALF + 1 : HALF + 2] + scale_g * (
            got[:, HALF + 1 : HALF + 2] + got[:, HALF + 2 : HALF + 3]
        )
        value = scale_k * kept[:, :HALF] + scale_g * got[:, :HALF]
        halves.append(with_stats(value, peak, *split_total(total)).reshape(8, 8, WIDE))
    first, second = halves
    top = lax.broadcasted_iota(jnp.int32, first.shape, 1) < 4
    even = jnp.where(top, first, pltpu.roll(second, 4, 1)).astype(BF16)
    odd = jnp.where(top, pltpu.roll(first, 4, 1), second).astype(BF16)
    for j in range(8):
        for x in range(4):
            out_ref[8 * j + x] = even[j]
            out_ref[8 * j + 4 + x] = odd[j]


def pack(keep, recv):
    return pl.pallas_call(
        pack_kernel,
        out_shape=jax.ShapeDtypeStruct((64, 8, WIDE), BF16),
        compiler_params=pltpu.CompilerParams(vmem_limit_bytes=24 << 20),
        name="pack",
    )(keep, recv)


def expert_kernel(own_ref, oth_ref, w_in_hbm, w_out_hbm, send_ref, keep_ref, w_in, w_out, inputs, pre, out, sems):
    core = lax.axis_index("core")
    mine = pl.ds(pl.multiple_of(core * HALF, 128), HALF)
    other = pl.ds(pl.multiple_of((1 - core) * HALF, 128), HALF)
    experts = w_in.shape[0]
    copies_in = [pltpu.make_async_copy(w_in_hbm.at[e], w_in.at[e], sems.at[0, e]) for e in range(experts)]
    copies_out = [pltpu.make_async_copy(w_out_hbm.at[e], w_out.at[e], sems.at[1, e]) for e in range(experts)]
    for copy in copies_in + copies_out:
        copy.start()
    for i in range(8):
        own = own_ref[8 * i : 8 * i + 8].astype(F32).reshape(2, 4, 8, WIDE)
        oth = oth_ref[8 * i : 8 * i + 8, :, :HALF].astype(F32).reshape(2, 4, 8, HALF)
        peaks = own[..., HALF : HALF + 1]
        weight = jnp.exp(peaks - jnp.max(peaks, axis=1, keepdims=True))
        total = jnp.sum(weight * (own[..., HALF + 1 : HALF + 2] + own[..., HALF + 2 : HALF + 3]), axis=1, keepdims=True)
        weight = weight / total
        rows = pl.ds(16 * i, 16)
        inputs[rows, mine] = jnp.sum(weight * own[..., :HALF], axis=1).reshape(16, HALF).astype(BF16)
        inputs[rows, other] = jnp.sum(weight * oth, axis=1).reshape(16, HALF).astype(BF16)
    slot = lax.broadcasted_iota(jnp.int32, (128, 1), 0) % 4
    for e in range(experts):
        copies_in[e].wait()
        here = jnp.dot(inputs[...], w_in[e], preferred_element_type=F32)
        pre[...] = here if e == 0 else jnp.where(slot == e, here, pre[...])
    value = pre[...]
    hidden = (0.5 * value * (1.0 + lax.erf(value * np.float32(np.sqrt(0.5))))).astype(BF16)
    for e in range(experts):
        copies_out[e].wait()
        here = jnp.dot(hidden, w_out[e], preferred_element_type=F32)
        out[...] = here if e == 0 else jnp.where(slot == e, here, out[...])
    send_ref[...] = out[:, other].astype(BF16)
    keep_ref[...] = out[:, mine]


def expert(own, oth, w_in, w_out):
    experts, width, hidden = w_in.shape
    vmem = pl.BlockSpec(memory_space=pltpu.VMEM)
    hbm = pl.BlockSpec(memory_space=pl.ANY)
    return pl.pallas_call(
        expert_kernel,
        out_shape=[jax.ShapeDtypeStruct((128, HALF), BF16), jax.ShapeDtypeStruct((128, HALF), F32)],
        in_specs=[vmem, vmem, hbm, hbm],
        out_specs=[vmem, vmem],
        scratch_shapes=[
            pltpu.VMEM(w_in.shape, BF16),
            pltpu.VMEM(w_out.shape, BF16),
            pltpu.VMEM((128, width), BF16),
            pltpu.VMEM((128, hidden), F32),
            pltpu.VMEM((128, width), F32),
            pltpu.SemaphoreType.DMA((2, experts)),
        ],
        compiler_params=pltpu.CompilerParams(vmem_limit_bytes=48 << 20),
        name="expert",
    )(own, oth, w_in, w_out)


def combine_kernel(logits_ref, out_ref):
    for b in range(2):
        logits = logits_ref[b]
        expd = jnp.exp(logits - jnp.max(logits, axis=0, keepdims=True))
        combine = expd / jnp.sum(expd, axis=0, keepdims=True)
        out_ref[b] = combine.T.astype(BF16)


def combine(logits):
    clips, slots, count = logits.shape
    return pl.pallas_call(
        combine_kernel,
        out_shape=jax.ShapeDtypeStruct((clips, count, slots), BF16),
        compiler_params=pltpu.CompilerParams(vmem_limit_bytes=24 << 20),
        cost_estimate=pl.CostEstimate(flops=8 * logits.size, bytes_accessed=6 * logits.size, transcendentals=logits.size),
        name="combine",
    )(logits)


def mix_kernel(combine_ref, own_ref, oth_ref, out_ref, outputs):
    @pl.when((pl.program_id(0) == 0) & (pl.program_id(1) == 0))
    def _():
        core = lax.axis_index("core")
        mine = pl.ds(pl.multiple_of(core * HALF, 128), HALF)
        other = pl.ds(pl.multiple_of((1 - core) * HALF, 128), HALF)
        top = lax.broadcasted_iota(jnp.int32, (2, 8, HALF), 1) < 4
        for ref, lanes in ((own_ref, mine), (oth_ref, other)):
            for i in range(4):
                part = ref[16 * i : 16 * i + 16].astype(F32).reshape(4, 4, 8, HALF)
                part = jnp.sum(part, axis=1).reshape(2, 2, 8, HALF)
                even, odd = part[:, 0], part[:, 1]
                first = jnp.where(top, even, pltpu.roll(odd, 4, 1))
                second = jnp.where(top, pltpu.roll(even, 4, 1), odd)
                rows = pl.ds(16 * i, 16)
                outputs[0, rows, lanes] = first.reshape(16, HALF).astype(BF16)
                outputs[1, rows, lanes] = second.reshape(16, HALF).astype(BF16)

    mixed = jnp.dot(combine_ref[0], outputs[pl.program_id(0)], preferred_element_type=F32)
    out_ref[0] = mixed.astype(BF16)


def mix(weights, own, oth):
    clips, count, slots = weights.shape
    rows = 512
    width = 2 * HALF
    return pl.pallas_call(
        mix_kernel,
        out_shape=jax.ShapeDtypeStruct((clips, count, width), BF16),
        grid=(clips, count // rows),
        in_specs=[
            pl.BlockSpec((1, rows, slots), lambda b, i: (b, i, 0)),
            pl.BlockSpec(own.shape, lambda b, i: (0, 0, 0)),
            pl.BlockSpec(own.shape, lambda b, i: (0, 0, 0)),
        ],
        out_specs=pl.BlockSpec((1, rows, width), lambda b, i: (b, i, 0)),
        scratch_shapes=[pltpu.VMEM((clips, slots, width), BF16)],
        compiler_params=pltpu.CompilerParams(vmem_limit_bytes=32 << 20),
        name="mix",
    )(weights, own, oth)


def swap(x):
    return lax.ppermute(x, "core", [(0, 1), (1, 0)])


def exchange(x):
    return lax.all_to_all(x, ("dp", "x"), 0, 0, tiled=True)


def on_device(tokens, slot_param, w_in, w_out):
    send, keep, logits = gather(tokens, slot_param.T)
    own = exchange(pack(keep, swap(send)))
    weights = combine(logits)
    send, keep = expert(own, swap(own), w_in, w_out)
    summed = (keep + swap(send).astype(F32)).astype(BF16).reshape(16, 1, 8, HALF)
    own = exchange(jnp.broadcast_to(summed, (16, 4, 8, HALF)).reshape(64, 8, HALF))
    return mix(weights, own, swap(own))


def solution(mesh):
    ctx = ("x", "core")
    split = jax.sharding.Mesh(np.asarray(mesh.devices).reshape(16, 4, 2), ("dp",) + ctx)
    placed = (P("dp", ctx, None), P(), P("dp", None, ctx), P("dp", ctx, None))
    return jax.shard_map(
        on_device, mesh=split, in_specs=placed, out_specs=P("dp", ctx, None), check_vma=False
    )
```

time: 175 us -> 75.8 us (0.43); the launches traced: 172 us -> 75.6 us
  waiting for transfers between devices: 56.2 us -> 5.45 us
  blocking collectives: 74.3 us -> 44.3 us
  matrix products: 20 us -> 0 us
  Pallas kernels: 0 us -> 16.6 us
  between operations: 13.4 us -> 0.05 us
  starting transfers between devices: 3.6 us -> 5.7 us
    psum x2 -> x0, blocking collectives: 46.8 us -> none  [the longest x1 32.1 us: on_device(): expert_out = lax.psum(returned, 'ctx').astype(jnp.bfloat16)]
    psum x1 -> x0, waiting for transfers between devices: 46.6 us -> none  [on_device(): total, whole = lax.psum((local_total, partial_value), 'ctx')]
    all_to_all x1 -> x2, blocking collectives: 14.3 us -> 44.3 us  [exchange(): return lax.all_to_all(x, ('dp', 'x'), 0, 0, tiled=True)]
    dot_general x4 -> x0, matrix products: 20 us -> none  [the longest x1 7.38 us: on_device(): jnp.einsum('bef,efd->bed', hidden, w_out, preferred_element_type=jnp.floa...]
    pallas_call x0 -> x5, Pallas kernels: none -> 16.6 us  [the longest x1 6.89 us: gather(): pl.pallas_call(functools.partial(gather_kernel, pieces), out_shape=[jax.S...]
    pmax x1 -> x0, blocking collectives: 13.2 us -> none  [on_device(): peak = lax.pmax(local_top, 'ctx')]
    all_to_all x1 -> x0, waiting for transfers between devices: 9.6 us -> none  [on_device(): lax.all_to_all(partial_out, 'dp', split_axis=0, concat_axis=1, tiled=True)]
    ppermute x0 -> x4, starting transfers between devices: none -> 5.7 us  [swap(): return lax.ppermute(x, 'core', [(0, 1), (1, 0)])]
  transfers between devices with their start and end apart: 2 -> 4, of which waited for: 2 -> 4; matrix products, arithmetic and copies ran while one was open for 0% -> 0% of each run, Pallas kernels for 0% -> 0%
where the time goes in v1:
time: 75.8 us; the launch traced here: 75.6 us
  blocking collectives  44.3 us (58%)
  Pallas kernels  16.6 us (22%)
  starting transfers between devices  5.7 us (8%)
  waiting for transfers between devices  5.45 us (7%)
  local copies, waits for them, and re-layouts  3.45 us (5%)
    all_to_all x2, blocking collectives, exchange(): return lax.all_to_all(x, ('dp', 'x'), 0, 0, tiled=True)  44.3 us
    pallas_call x1, Pallas kernels, gather(): pl.pallas_call(functools.partial(gather_kernel, pieces), out_shape=[jax.S...  6.89 us
    ppermute x4, starting transfers between devices, swap(): return lax.ppermute(x, 'core', [(0, 1), (1, 0)])  5.7 us
    ppermute x4, waiting for transfers between devices, swap(): return lax.ppermute(x, 'core', [(0, 1), (1, 0)])  5.45 us
    pallas_call x1, Pallas kernels, expert(): pl.pallas_call(expert_kernel, out_shape=[jax.ShapeDtypeStruct((128, HALF)...  5.44 us
    pallas_call x1, Pallas kernels, mix(): pl.pallas_call(mix_kernel, out_shape=jax.ShapeDtypeStruct((clips, count,...  3.77 us
    unnamed x4, local copies, waits for them, and re-layouts  3.4 us
  transfers between devices with their start and end apart: 4, of which 4 were waited for; matrix products, arithmetic and copies ran while one was open for 0% of the time, Pallas kernels for 0%

profile of v1, /device:TPU:1, one launch (start us, length us, event | category | flops | bytes accessed | tf_op | source)
XLA Modules:
  0.0 75.6 jit_solution(1810265922868974040)
XLA Ops:
  0.0 0.0 copy-start
  0.0 2.5 %copy-done = bf16[2,1024,1280]{2,1,0:T(8,128)(2,1)S(1)} copy-done((bf16[2,1024,1280]{2,1,0:T(8,128)(2,1)S(1)}, bf16[2,1024,1280]{2,1,0:T(8,128)(2,1)}, u32[]{:S(2)}) %copy-start) | copy-done | bytes 5242904
  2.5 0.0 copy-start.1
  2.5 0.9 %copy-done.1 = bf16[1280,64]{0,1:T(8,128)(2,1)S(1)} copy-done((bf16[1280,64]{0,1:T(8,128)(2,1)S(1)}, bf16[1280,64]{0,1:T(8,128)(2,1)}, u32[]{:S(2)}) %copy-start.1) | copy-done | bytes 163864
  3.4 6.9 %gather.1 = (bf16[2,64,768]{2,1,0:T(8,128)(2,1)S(1)}, f32[2,64,768]{2,1,0:T(8,128)S(1)}, f32[2,64,1024]{2,1,0:T(8,128)S(1)}) custom-call(bf16[2,1024,1280]{2,1,0:T(8,128)(2,1)S(1)} %copy-done, bf16[64,1280]{1,0:T(8,128)(2,1)S(1)} %bitcast.4), custom_call_target="tpu_custom_call" | custom-call | flops 671088640 | bytes 5242880 | tf_op jit(solution)/shard_map/gather/pallas_call | solution.py:63
  10.3 1.5 %collective-permute-start = (bf16[2,64,768]{2,1,0:T(8,128)(2,1)S(1)}, bf16[2,64,768]{2,1,0:T(8,128)(2,1)S(1)}, u32[]{:S(2)}, u32[]{:S(2)}) collective-permute-start(bf16[2,64,768]{2,1,0:T(8,128)(2,1)S(1)} %get-tuple-element.12), channel_id=1, source_target_pairs={{0,1},{1,0},{2,3},{3,2},{4,5},{5,4},{6,7},{7,6},{8,9},{9,8},{10,11... | collective-permute-start | bytes 589832 | tf_op jit(solution)/shard_map/ppermute | solution.py:236
  11.8 1.1 %collective-permute-done.recv_ref = bf16[2,64,768]{2,1,0:T(8,128)(2,1)S(1)} collective-permute-done((bf16[2,64,768]{2,1,0:T(8,128)(2,1)S(1)}, bf16[2,64,768]{2,1,0:T(8,128)(2,1)S(1)}, u32[]{:S(2)}, u32[]{:S(2)}) %collective-permute-start) | collective-permute-done | bytes 196640 | tf_op jit(solution)/shard_map/ppermute | solution.py:236
  12.9 0.3 pack.1
  13.2 26.3 %all_to_all.10.own_ref = bf16[64,8,768]{2,1,0:T(8,128)(2,1)S(1)} all-to-all(bf16[64,8,768]{2,1,0:T(8,128)(2,1)S(1)} %pack.1), channel_id=1, replica_groups=mesh['dp'=16,'x'=4,'core'=2] {'dp','x'}, dimensions={0} | all-to-all | bytes 1572864 | tf_op jit(solution)/shard_map/all_to_all | solution.py:240
  39.4 1.9 %collective-permute-start.1 = (bf16[64,8,768]{2,1,0:T(8,128)(2,1)S(1)}, bf16[64,8,768]{2,1,0:T(8,128)(2,1)S(1)}, u32[]{:S(2)}, u32[]{:S(2)}) collective-permute-start(bf16[64,8,768]{2,1,0:T(8,128)(2,1)S(1)} %all_to_all.10.own_ref), channel_id=1, source_target_pairs={{0,1},{1,0},{2,3},{3,2},{4,5},{5,4},{6,7},{7,6},{8,9},{9,8},{10,11... | collective-permute-start | bytes 2359304 | tf_op jit(solution)/shard_map/ppermute | solution.py:236
  41.3 1.9 %collective-permute-done.1.oth_ref = bf16[64,8,768]{2,1,0:T(8,128)(2,1)S(1)} collective-permute-done((bf16[64,8,768]{2,1,0:T(8,128)(2,1)S(1)}, bf16[64,8,768]{2,1,0:T(8,128)(2,1)S(1)}, u32[]{:S(2)}, u32[]{:S(2)}) %collective-permute-start.1) | collective-permute-done | bytes 786464 | tf_op jit(solution)/shard_map/ppermute | solution.py:236
  43.2 5.4 %expert.1 = (bf16[128,640]{1,0:T(8,128)(2,1)S(1)}, f32[128,640]{1,0:T(8,128)S(1)}) custom-call(bf16[64,8,768]{2,1,0:T(8,128)(2,1)S(1)} %all_to_all.10.own_ref, bf16[64,8,768]{2,1,0:T(8,128)(2,1)S(1)} %collective-permute-done.1.oth_ref, bf16[4,1280,640]{2,1,0:T(8,128)(2,1)} %w_in_hbm.1, bf16[4,640,1280]{2,1,0:T(8,128)(2,1)} %w_out_hbm.1), custom_call_target="tpu_custom_call" | custom-call | tf_op jit(solution)/shard_map/expert/pallas_call | solution.py:156
  48.7 0.5 collective-permute-start.2
  49.1 1.0 %collective-permute-done.2 = bf16[128,640]{1,0:T(8,128)(2,1)S(1)} collective-permute-done((bf16[128,640]{1,0:T(8,128)(2,1)S(1)}, bf16[128,640]{1,0:T(8,128)(2,1)S(1)}, u32[]{:S(2)}, u32[]{:S(2)}) %collective-permute-start.2) | collective-permute-done | bytes 163872 | tf_op jit(solution)/shard_map/ppermute | solution.py:236
  50.2 0.1 broadcast_in_dim.8
  50.3 18.0 %all_to_all.11.own_ref = bf16[64,8,640]{2,1,0:T(8,128)(2,1)S(1)} all-to-all(bf16[64,8,640]{2,1,0:T(8,128)(2,1)S(1)} %bitcast.5), channel_id=1, replica_groups=mesh['dp'=16,'x'=4,'core'=2] {'dp','x'}, dimensions={0} | all-to-all | bytes 1310720 | tf_op jit(solution)/shard_map/all_to_all | solution.py:240
  68.3 1.8 %collective-permute-start.3 = (bf16[64,8,640]{2,1,0:T(8,128)(2,1)S(1)}, bf16[64,8,640]{2,1,0:T(8,128)(2,1)S(1)}, u32[]{:S(2)}, u32[]{:S(2)}) collective-permute-start(bf16[64,8,640]{2,1,0:T(8,128)(2,1)S(1)} %all_to_all.11.own_ref), channel_id=1, source_target_pairs={{0,1},{1,0},{2,3},{3,2},{4,5},{5,4},{6,7},{7,6},{8,9},{9,8},{10,11... | collective-permute-start | bytes 1966088 | tf_op jit(solution)/shard_map/ppermute | solution.py:236
  70.1 0.3 combine.1.combine_ref
  70.4 1.4 %collective-permute-done.3.oth_ref = bf16[64,8,640]{2,1,0:T(8,128)(2,1)S(1)} collective-permute-done((bf16[64,8,640]{2,1,0:T(8,128)(2,1)S(1)}, bf16[64,8,640]{2,1,0:T(8,128)(2,1)S(1)}, u32[]{:S(2)}, u32[]{:S(2)}) %collective-permute-start.3) | collective-permute-done | bytes 655392 | tf_op jit(solution)/shard_map/ppermute | solution.py:236
  71.8 3.8 %mix.1 = bf16[2,1024,1280]{2,1,0:T(8,128)(2,1)} custom-call(bf16[2,1024,64]{2,1,0:T(8,128)(2,1)S(1)} %combine.1.combine_ref, bf16[64,8,640]{2,1,0:T(8,128)(2,1)S(1)} %all_to_all.11.own_ref, bf16[64,8,640]{2,1,0:T(8,128)(2,1)S(1)} %collective-permute-done.3.oth_ref), custom_call_target="tpu_custom_call" | custom-call | tf_op jit(solution)/shard_map/mix/pallas_call | solution.py:219
  (1 shorter events, 0.0 us)
Async XLA Ops:
  0.0 2.5 %copy-start = (bf16[2,1024,1280]{2,1,0:T(8,128)(2,1)S(1)}, bf16[2,1024,1280]{2,1,0:T(8,128)(2,1)}, u32[]{:S(2)}) copy-start(bf16[2,1024,1280]{2,1,0:T(8,128)(2,1)} %tokens_hbm.1) | copy-start | bytes 15728644
  2.5 0.9 %copy-start.1 = (bf16[1280,64]{0,1:T(8,128)(2,1)S(1)}, bf16[1280,64]{0,1:T(8,128)(2,1)}, u32[]{:S(2)}) copy-start(bf16[1280,64]{0,1:T(8,128)(2,1)} %param.5) | copy-start | bytes 491524
  10.3 2.6 %collective-permute-start = (bf16[2,64,768]{2,1,0:T(8,128)(2,1)S(1)}, bf16[2,64,768]{2,1,0:T(8,128)(2,1)S(1)}, u32[]{:S(2)}, u32[]{:S(2)}) collective-permute-start(bf16[2,64,768]{2,1,0:T(8,128)(2,1)S(1)} %get-tuple-element.12), channel_id=1, source_target_pairs={{0,1},{1,0},{2,3},{3,2},{4,5},{5,4},{6,7},{7,6},{8,9},{9,8},{10,11... | collective-permute-start | bytes 589832 | tf_op jit(solution)/shard_map/ppermute | solution.py:236
  39.4 3.8 %collective-permute-start.1 = (bf16[64,8,768]{2,1,0:T(8,128)(2,1)S(1)}, bf16[64,8,768]{2,1,0:T(8,128)(2,1)S(1)}, u32[]{:S(2)}, u32[]{:S(2)}) collective-permute-start(bf16[64,8,768]{2,1,0:T(8,128)(2,1)S(1)} %all_to_all.10.own_ref), channel_id=1, source_target_pairs={{0,1},{1,0},{2,3},{3,2},{4,5},{5,4},{6,7},{7,6},{8,9},{9,8},{10,11... | collective-permute-start | bytes 2359304 | tf_op jit(solution)/shard_map/ppermute | solution.py:236
  48.7 1.5 %collective-permute-start.2 = (bf16[128,640]{1,0:T(8,128)(2,1)S(1)}, bf16[128,640]{1,0:T(8,128)(2,1)S(1)}, u32[]{:S(2)}, u32[]{:S(2)}) collective-permute-start(bf16[128,640]{1,0:T(8,128)(2,1)S(1)} %get-tuple-element.14), channel_id=1, source_target_pairs={{0,1},{1,0},{2,3},{3,2},{4,5},{5,4},{6,7},{7,6},{8,9},{9,8},{10,11... | collective-permute-start | bytes 491528 | tf_op jit(solution)/shard_map/ppermute | solution.py:236
  68.3 3.6 %collective-permute-start.3 = (bf16[64,8,640]{2,1,0:T(8,128)(2,1)S(1)}, bf16[64,8,640]{2,1,0:T(8,128)(2,1)S(1)}, u32[]{:S(2)}, u32[]{:S(2)}) collective-permute-start(bf16[64,8,640]{2,1,0:T(8,128)(2,1)S(1)} %all_to_all.11.own_ref), channel_id=1, source_target_pairs={{0,1},{1,0},{2,3},{3,2},{4,5},{5,4},{6,7},{7,6},{8,9},{9,8},{10,11... | collective-permute-start | bytes 1966088 | tf_op jit(solution)/shard_map/ppermute | solution.py:236

commit v2 on v1

--- a/solution.py
+++ b/solution.py
@@ -26,7 +26,7 @@
     return high, total - high
 
 
-def gather_kernel(pieces, tokens_hbm, slots_ref, send_ref, keep_ref, logits_ref, tokens, whole, sems):
+def gather_kernel(pieces, tokens_hbm, slots_hbm, send_ref, keep_ref, logits_ref, tokens, slots_ref, whole, sems):
     core = lax.axis_index("core")
     mine = pl.ds(pl.multiple_of(core * HALF, 128), HALF)
     other = pl.ds(pl.multiple_of((1 - core) * HALF, 128), HALF)
@@ -37,9 +37,12 @@
         rows = pl.ds(i * step, step)
         return pltpu.make_async_copy(tokens_hbm.at[b, rows], tokens.at[b, rows], sems.at[b, i])
 
+    slots_copy = pltpu.make_async_copy(slots_hbm, slots_ref, sems.at[clips, 0])
+    slots_copy.start()
     for b in range(clips):
         for i in range(pieces):
             copy(b, i).start()
+    slots_copy.wait()
     for b in range(clips):
         for i in range(pieces):
             copy(b, i).wait()
@@ -59,22 +62,23 @@
 def gather(tokens, slots_t):
     clips, count, width = tokens.shape
     slots = slots_t.shape[0]
-    pieces = 4
+    pieces = 2
     return pl.pallas_call(
         functools.partial(gather_kernel, pieces),
         out_shape=[
-            jax.ShapeDtypeStruct((clips, slots, WIDE), BF16),
-            jax.ShapeDtypeStruct((clips, slots, WIDE), F32),
-            jax.ShapeDtypeStruct((clips, slots, count), F32),
-        ],
-        in_specs=[pl.BlockSpec(memory_space=pl.ANY), pl.BlockSpec(memory_space=pltpu.VMEM)],
+            pltpu.VMEM((clips, slots, WIDE), BF16),
+            pltpu.VMEM((clips, slots, WIDE), F32),
+            pltpu.VMEM((clips, slots, count), F32),
+        ],
+        in_specs=[pl.BlockSpec(memory_space=pl.ANY)] * 2,
         out_specs=[pl.BlockSpec(memory_space=pltpu.VMEM)] * 3,
         scratch_shapes=[
             pltpu.VMEM((clips, count, width), BF16),
+            pltpu.VMEM((slots, width), BF16),
             pltpu.VMEM((slots, width), F32),
-            pltpu.SemaphoreType.DMA((clips, pieces)),
-        ],
-        compiler_params=pltpu.CompilerParams(vmem_limit_bytes=40 << 20),
+            pltpu.SemaphoreType.DMA((clips + 1, pieces)),
+        ],
+        compiler_params=pltpu.CompilerParams(vmem_limit_bytes=62 << 20),
         cost_estimate=pl.CostEstimate(
             flops=4 * clips * slots * count * width,
             bytes_accessed=2 * clips * count * width,
@@ -111,38 +115,45 @@
         pack_kernel,
         out_shape=jax.ShapeDtypeStruct((64, 8, WIDE), BF16),
         compiler_params=pltpu.CompilerParams(vmem_limit_bytes=24 << 20),
+        cost_estimate=pl.CostEstimate(flops=1 << 36, bytes_accessed=100 << 20, transcendentals=0),
         name="pack",
     )(keep, recv)
 
 
-def expert_kernel(own_ref, oth_ref, w_in_hbm, w_out_hbm, send_ref, keep_ref, w_in, w_out, inputs, pre, out, sems):
+def reduce_kernel(parts_ref, out_ref):
+    for i in range(8):
+        part = parts_ref[8 * i : 8 * i + 8].astype(F32).reshape(2, 4, 8, WIDE)
+        peak = part[..., HALF : HALF + 1]
+        weight = jnp.exp(peak - jnp.max(peak, axis=1, keepdims=True))
+        total = weight * (part[..., HALF + 1 : HALF + 2] + part[..., HALF + 2 : HALF + 3])
+        weight = weight / jnp.sum(total, axis=1, keepdims=True)
+        slot_in = jnp.sum(weight * part[..., :HALF], axis=1)
+        out_ref[pl.ds(16 * i, 16), :] = slot_in.reshape(16, HALF).astype(BF16)
+
+
+def reduce(parts):
+    return pl.pallas_call(
+        reduce_kernel,
+        out_shape=jax.ShapeDtypeStruct((128, HALF), BF16),
+        compiler_params=pltpu.CompilerParams(vmem_limit_bytes=24 << 20),
+        name="reduce",
+    )(parts)
+
+
+def expert_kernel(own_ref, oth_ref, w_in, w_out, send_ref, keep_ref, inputs, pre, out):
     core = lax.axis_index("core")
     mine = pl.ds(pl.multiple_of(core * HALF, 128), HALF)
     other = pl.ds(pl.multiple_of((1 - core) * HALF, 128), HALF)
     experts = w_in.shape[0]
-    copies_in = [pltpu.make_async_copy(w_in_hbm.at[e], w_in.at[e], sems.at[0, e]) for e in range(experts)]
-    copies_out = [pltpu.make_async_copy(w_out_hbm.at[e], w_out.at[e], sems.at[1, e]) for e in range(experts)]
-    for copy in copies_in + copies_out:
-        copy.start()
-    for i in range(8):
-        own = own_ref[8 * i : 8 * i + 8].astype(F32).reshape(2, 4, 8, WIDE)
-        oth = oth_ref[8 * i : 8 * i + 8, :, :HALF].astype(F32).reshape(2, 4, 8, HALF)
-        peaks = own[..., HALF : HALF + 1]
-        weight = jnp.exp(peaks - jnp.max(peaks, axis=1, keepdims=True))
-        total = jnp.sum(weight * (own[..., HALF + 1 : HALF + 2] + own[..., HALF + 2 : HALF + 3]), axis=1, keepdims=True)
-        weight = weight / total
-        rows = pl.ds(16 * i, 16)
-        inputs[rows, mine] = jnp.sum(weight * own[..., :HALF], axis=1).reshape(16, HALF).astype(BF16)
-        inputs[rows, other] = jnp.sum(weight * oth, axis=1).reshape(16, HALF).astype(BF16)
+    inputs[:, mine] = own_ref[...]
+    inputs[:, other] = oth_ref[...]
     slot = lax.broadcasted_iota(jnp.int32, (128, 1), 0) % 4
     for e in range(experts):
-        copies_in[e].wait()
         here = jnp.dot(inputs[...], w_in[e], preferred_element_type=F32)
         pre[...] = here if e == 0 else jnp.where(slot == e, here, pre[...])
     value = pre[...]
     hidden = (0.5 * value * (1.0 + lax.erf(value * np.float32(np.sqrt(0.5))))).astype(BF16)
     for e in range(experts):
-        copies_out[e].wait()
         here = jnp.dot(hidden, w_out[e], preferred_element_type=F32)
         out[...] = here if e == 0 else jnp.where(slot == e, here, out[...])
     send_ref[...] = out[:, other].astype(BF16)
@@ -152,21 +163,17 @@
 def expert(own, oth, w_in, w_out):
     experts, width, hidden = w_in.shape
     vmem = pl.BlockSpec(memory_space=pltpu.VMEM)
-    hbm = pl.BlockSpec(memory_space=pl.ANY)
     return pl.pallas_call(
         expert_kernel,
         out_shape=[jax.ShapeDtypeStruct((128, HALF), BF16), jax.ShapeDtypeStruct((128, HALF), F32)],
-        in_specs=[vmem, vmem, hbm, hbm],
+        in_specs=[vmem] * 4,
         out_specs=[vmem, vmem],
         scratch_shapes=[
-            pltpu.VMEM(w_in.shape, BF16),
-            pltpu.VMEM(w_out.shape, BF16),
             pltpu.VMEM((128, width), BF16),
             pltpu.VMEM((128, hidden), F32),
             pltpu.VMEM((128, width), F32),
-            pltpu.SemaphoreType.DMA((2, experts)),
-        ],
-        compiler_params=pltpu.CompilerParams(vmem_limit_bytes=48 << 20),
+        ],
+        compiler_params=pltpu.CompilerParams(vmem_limit_bytes=24 << 20),
         name="expert",
     )(own, oth, w_in, w_out)
 
@@ -190,26 +197,35 @@
     )(logits)
 
 
-def mix_kernel(combine_ref, own_ref, oth_ref, out_ref, outputs):
-    @pl.when((pl.program_id(0) == 0) & (pl.program_id(1) == 0))
-    def _():
-        core = lax.axis_index("core")
-        mine = pl.ds(pl.multiple_of(core * HALF, 128), HALF)
-        other = pl.ds(pl.multiple_of((1 - core) * HALF, 128), HALF)
-        top = lax.broadcasted_iota(jnp.int32, (2, 8, HALF), 1) < 4
-        for ref, lanes in ((own_ref, mine), (oth_ref, other)):
-            for i in range(4):
-                part = ref[16 * i : 16 * i + 16].astype(F32).reshape(4, 4, 8, HALF)
-                part = jnp.sum(part, axis=1).reshape(2, 2, 8, HALF)
-                even, odd = part[:, 0], part[:, 1]
-                first = jnp.where(top, even, pltpu.roll(odd, 4, 1))
-                second = jnp.where(top, pltpu.roll(even, 4, 1), odd)
-                rows = pl.ds(16 * i, 16)
-                outputs[0, rows, lanes] = first.reshape(16, HALF).astype(BF16)
-                outputs[1, rows, lanes] = second.reshape(16, HALF).astype(BF16)
-
-    mixed = jnp.dot(combine_ref[0], outputs[pl.program_id(0)], preferred_element_type=F32)
-    out_ref[0] = mixed.astype(BF16)
+def sum_kernel(parts_ref, out_ref):
+    top = lax.broadcasted_iota(jnp.int32, (2, 8, HALF), 1) < 4
+    for i in range(4):
+        part = parts_ref[16 * i : 16 * i + 16].astype(F32).reshape(4, 4, 8, HALF)
+        part = jnp.sum(part, axis=1).reshape(2, 2, 8, HALF)
+        even, odd = part[:, 0], part[:, 1]
+        first = jnp.where(top, even, pltpu.roll(odd, 4, 1))
+        second = jnp.where(top, pltpu.roll(even, 4, 1), odd)
+        rows = pl.ds(16 * i, 16)
+        out_ref[0, rows] = first.reshape(16, HALF).astype(BF16)
+        out_ref[1, rows] = second.reshape(16, HALF).astype(BF16)
+
+
+def sum_parts(parts):
+    return pl.pallas_call(
+        sum_kernel,
+        out_shape=jax.ShapeDtypeStruct((2, 64, HALF), BF16),
+        compiler_params=pltpu.CompilerParams(vmem_limit_bytes=24 << 20),
+        name="sum_parts",
+    )(parts)
+
+
+def mix_kernel(combine_ref, own_ref, oth_ref, out_ref):
+    core = lax.axis_index("core")
+    mine = pl.ds(pl.multiple_of(core * HALF, 128), HALF)
+    other = pl.ds(pl.multiple_of((1 - core) * HALF, 128), HALF)
+    weights = combine_ref[0]
+    out_ref[0, :, mine] = jnp.dot(weights, own_ref[0], preferred_element_type=F32).astype(BF16)
+    out_ref[0, :, other] = jnp.dot(weights, oth_ref[0], preferred_element_type=F32).astype(BF16)
 
 
 def mix(weights, own, oth):
@@ -222,11 +238,10 @@
         grid=(clips, count // rows),
         in_specs=[
             pl.BlockSpec((1, rows, slots), lambda b, i: (b, i, 0)),
-            pl.BlockSpec(own.shape, lambda b, i: (0, 0, 0)),
-            pl.BlockSpec(own.shape, lambda b, i: (0, 0, 0)),
+            pl.BlockSpec((1, slots, HALF), lambda b, i: (b, 0, 0)),
+            pl.BlockSpec((1, slots, HALF), lambda b, i: (b, 0, 0)),
         ],
         out_specs=pl.BlockSpec((1, rows, width), lambda b, i: (b, i, 0)),
-        scratch_shapes=[pltpu.VMEM((clips, slots, width), BF16)],
         compiler_params=pltpu.CompilerParams(vmem_limit_bytes=32 << 20),
         name="mix",
     )(weights, own, oth)
@@ -241,12 +256,15 @@
 
 
 def on_device(tokens, slot_param, w_in, w_out):
-    send, keep, logits = gather(tokens, slot_param.T)
-    own = exchange(pack(keep, swap(send)))
+    send, keep, logits = gather(
+        pltpu.with_memory_space_constraint(tokens, pltpu.HBM),
+        pltpu.with_memory_space_constraint(slot_param.T, pltpu.HBM),
+    )
+    own = reduce(exchange(pack(keep, swap(send))))
     weights = combine(logits)
     send, keep = expert(own, swap(own), w_in, w_out)
     summed = (keep + swap(send).astype(F32)).astype(BF16).reshape(16, 1, 8, HALF)
-    own = exchange(jnp.broadcast_to(summed, (16, 4, 8, HALF)).reshape(64, 8, HALF))
+    own = sum_parts(exchange(jnp.broadcast_to(summed, (16, 4, 8, HALF)).reshape(64, 8, HALF)))
     return mix(weights, own, swap(own))
 
 

time: 75.8 us -> 66.5 us (0.88)
  Pallas kernels: 16.6 us -> 11.9 us
  local copies, waits for them, and re-layouts: 3.45 us -> 0.06 us
  waiting for transfers between devices: 5.45 us -> 3.87 us
    unnamed x4, local copies, waits for them, and re-layouts: 3.4 us -> 0.01 us
    pallas_call x1, Pallas kernels: 5.44 us -> 2.36 us  [expert(): pl.pallas_call(expert_kernel, out_shape=[jax.ShapeDtypeStruct((128, HALF)...]
    ppermute x4, waiting for transfers between devices: 5.45 us -> 3.87 us  [swap(): return lax.ppermute(x, 'core', [(0, 1), (1, 0)])]
    pallas_call x1 -> x3, Pallas kernels: 6.89 us -> 5.45 us  [the longest x1 4.97 us: gather(): pl.pallas_call(functools.partial(gather_kernel, pieces), out_shape=[pltpu...]
where the time goes in v2:
time: 66.5 us; the launch traced here: 66.3 us
  blocking collectives  44.5 us (67%)
  Pallas kernels  11.9 us (18%)
  starting transfers between devices  5.86 us (9%)
  waiting for transfers between devices  3.87 us (6%)
    all_to_all x2, blocking collectives, exchange(): return lax.all_to_all(x, ('dp', 'x'), 0, 0, tiled=True)  44.5 us
    ppermute x4, starting transfers between devices, swap(): return lax.ppermute(x, 'core', [(0, 1), (1, 0)])  5.86 us
    pallas_call x1, Pallas kernels, gather(): pl.pallas_call(functools.partial(gather_kernel, pieces), out_shape=[pltpu...  4.97 us
    ppermute x4, waiting for transfers between devices, swap(): return lax.ppermute(x, 'core', [(0, 1), (1, 0)])  3.87 us
    pallas_call x1, Pallas kernels, mix(): pl.pallas_call(mix_kernel, out_shape=jax.ShapeDtypeStruct((clips, count,...  3.55 us
    pallas_call x1, Pallas kernels, expert(): pl.pallas_call(expert_kernel, out_shape=[jax.ShapeDtypeStruct((128, HALF)...  2.36 us
  transfers between devices with their start and end apart: 4, of which 4 were waited for; matrix products, arithmetic and copies ran while one was open for 0% of the time, Pallas kernels for 0%

profile of v2, /device:TPU:1, one launch (start us, length us, event | category | flops | bytes accessed | tf_op | source)
XLA Modules:
  0.0 66.3 jit_solution(4675141765851875513)
XLA Ops:
  0.0 5.0 %gather.1 = (bf16[2,64,768]{2,1,0:T(8,128)(2,1)S(1)}, f32[2,64,768]{2,1,0:T(8,128)S(1)}, f32[2,64,1024]{2,1,0:T(8,128)S(1)}) custom-call(bf16[2,1024,1280]{2,1,0:T(8,128)(2,1)} %tokens_hbm.1, bf16[64,1280]{1,0:T(8,128)(2,1)} %bitcast.5), custom_call_target="tpu_custom_call" | custom-call | flops 671088640 | bytes 5242880 | tf_op jit(solution)/shard_map/gather/pallas_call | solution.py:66
  5.0 1.5 %collective-permute-start = (bf16[2,64,768]{2,1,0:T(8,128)(2,1)S(1)}, bf16[2,64,768]{2,1,0:T(8,128)(2,1)S(1)}, u32[]{:S(2)}, u32[]{:S(2)}) collective-permute-start(bf16[2,64,768]{2,1,0:T(8,128)(2,1)S(1)} %get-tuple-element.12), channel_id=1, source_target_pairs={{0,1},{1,0},{2,3},{3,2},{4,5},{5,4},{6,7},{7,6},{8,9},{9,8},{10,11... | collective-permute-start | bytes 589832 | tf_op jit(solution)/shard_map/ppermute | solution.py:251
  6.5 1.1 %collective-permute-done.recv_ref = bf16[2,64,768]{2,1,0:T(8,128)(2,1)S(1)} collective-permute-done((bf16[2,64,768]{2,1,0:T(8,128)(2,1)S(1)}, bf16[2,64,768]{2,1,0:T(8,128)(2,1)S(1)}, u32[]{:S(2)}, u32[]{:S(2)}) %collective-permute-start) | collective-permute-done | bytes 196640 | tf_op jit(solution)/shard_map/ppermute | solution.py:251
  7.5 0.0 copy-start
  7.5 0.0 copy-start.1
  7.6 0.3 pack.1
  7.8 26.5 %all_to_all.10.parts_ref = bf16[64,8,768]{2,1,0:T(8,128)(2,1)S(1)} all-to-all(bf16[64,8,768]{2,1,0:T(8,128)(2,1)S(1)} %pack.1), channel_id=1, replica_groups=mesh['dp'=16,'x'=4,'core'=2] {'dp','x'}, dimensions={0} | all-to-all | bytes 1572864 | tf_op jit(solution)/shard_map/all_to_all | solution.py:255
  34.4 0.4 reduce.1.own_ref
  34.7 2.0 %collective-permute-start.1 = (bf16[128,640]{1,0:T(8,128)(2,1)S(1)}, bf16[128,640]{1,0:T(8,128)(2,1)S(1)}, u32[]{:S(2)}, u32[]{:S(2)}) collective-permute-start(bf16[128,640]{1,0:T(8,128)(2,1)S(1)} %reduce.1.own_ref), channel_id=1, source_target_pairs={{0,1},{1,0},{2,3},{3,2},{4,5},{5,4},{6,7},{7,6},{8,9},{9,8},{10,11... | collective-permute-start | bytes 491528 | tf_op jit(solution)/shard_map/ppermute | solution.py:251
  36.7 1.0 %collective-permute-done.1.oth_ref = bf16[128,640]{1,0:T(8,128)(2,1)S(1)} collective-permute-done((bf16[128,640]{1,0:T(8,128)(2,1)S(1)}, bf16[128,640]{1,0:T(8,128)(2,1)S(1)}, u32[]{:S(2)}, u32[]{:S(2)}) %collective-permute-start.1) | collective-permute-done | bytes 163872 | tf_op jit(solution)/shard_map/ppermute | solution.py:251
  37.8 0.0 copy-done
  37.8 0.0 copy-done.1
  37.8 2.4 %expert.1 = (bf16[128,640]{1,0:T(8,128)(2,1)S(1)}, f32[128,640]{1,0:T(8,128)S(1)}) custom-call(bf16[128,640]{1,0:T(8,128)(2,1)S(1)} %reduce.1.own_ref, bf16[128,640]{1,0:T(8,128)(2,1)S(1)} %collective-permute-done.1.oth_ref, bf16[4,1280,640]{2,1,0:T(8,128)(2,1)S(1)} %copy-done, bf16[4,640,1280]{2,1,0:T(8,128)(2,1)S(1)} %copy-done.1), custom_call_target="tpu_custom_call" | custom-call | tf_op jit(solution)/shard_map/expert/pallas_call | solution.py:166
  40.1 0.5 collective-permute-start.2
  40.6 1.0 %collective-permute-done.2 = bf16[128,640]{1,0:T(8,128)(2,1)S(1)} collective-permute-done((bf16[128,640]{1,0:T(8,128)(2,1)S(1)}, bf16[128,640]{1,0:T(8,128)(2,1)S(1)}, u32[]{:S(2)}, u32[]{:S(2)}) %collective-permute-start.2) | collective-permute-done | bytes 163872 | tf_op jit(solution)/shard_map/ppermute | solution.py:251
  41.6 0.1 broadcast_in_dim.8
  41.7 18.0 %all_to_all.11.parts_ref = bf16[64,8,640]{2,1,0:T(8,128)(2,1)S(1)} all-to-all(bf16[64,8,640]{2,1,0:T(8,128)(2,1)S(1)} %bitcast.4), channel_id=1, replica_groups=mesh['dp'=16,'x'=4,'core'=2] {'dp','x'}, dimensions={0} | all-to-all | bytes 1310720 | tf_op jit(solution)/shard_map/all_to_all | solution.py:255
  59.7 0.1 sum_parts.1.own_ref
  59.8 1.9 %collective-permute-start.3 = (bf16[2,64,640]{2,1,0:T(8,128)(2,1)S(1)}, bf16[2,64,640]{2,1,0:T(8,128)(2,1)S(1)}, u32[]{:S(2)}, u32[]{:S(2)}) collective-permute-start(bf16[2,64,640]{2,1,0:T(8,128)(2,1)S(1)} %sum_parts.1.own_ref), channel_id=1, source_target_pairs={{0,1},{1,0},{2,3},{3,2},{4,5},{5,4},{6,7},{7,6},{8,9},{9,8},{10,11... | collective-permute-start | bytes 491528 | tf_op jit(solution)/shard_map/ppermute | solution.py:251
  61.7 0.3 combine.1.combine_ref
  62.0 0.7 %collective-permute-done.3.oth_ref = bf16[2,64,640]{2,1,0:T(8,128)(2,1)S(1)} collective-permute-done((bf16[2,64,640]{2,1,0:T(8,128)(2,1)S(1)}, bf16[2,64,640]{2,1,0:T(8,128)(2,1)S(1)}, u32[]{:S(2)}, u32[]{:S(2)}) %collective-permute-start.3) | collective-permute-done | bytes 163872 | tf_op jit(solution)/shard_map/ppermute | solution.py:251
  62.8 3.6 %mix.1 = bf16[2,1024,1280]{2,1,0:T(8,128)(2,1)} custom-call(bf16[2,1024,64]{2,1,0:T(8,128)(2,1)S(1)} %combine.1.combine_ref, bf16[2,64,640]{2,1,0:T(8,128)(2,1)S(1)} %sum_parts.1.own_ref, bf16[2,64,640]{2,1,0:T(8,128)(2,1)S(1)} %collective-permute-done.3.oth_ref), custom_call_target="tpu_custom_call" | custom-call | tf_op jit(solution)/shard_map/mix/pallas_call | solution.py:235
  (1 shorter events, 0.0 us)
Async XLA Ops:
  5.0 2.6 %collective-permute-start = (bf16[2,64,768]{2,1,0:T(8,128)(2,1)S(1)}, bf16[2,64,768]{2,1,0:T(8,128)(2,1)S(1)}, u32[]{:S(2)}, u32[]{:S(2)}) collective-permute-start(bf16[2,64,768]{2,1,0:T(8,128)(2,1)S(1)} %get-tuple-element.12), channel_id=1, source_target_pairs={{0,1},{1,0},{2,3},{3,2},{4,5},{5,4},{6,7},{7,6},{8,9},{9,8},{10,11... | collective-permute-start | bytes 589832 | tf_op jit(solution)/shard_map/ppermute | solution.py:251
  7.5 30.2 %copy-start = (bf16[4,1280,640]{2,1,0:T(8,128)(2,1)S(1)}, bf16[4,1280,640]{2,1,0:T(8,128)(2,1)}, u32[]{:S(2)}) copy-start(bf16[4,1280,640]{2,1,0:T(8,128)(2,1)} %w_in.1) | copy-start | bytes 19660804
  7.5 30.2 %copy-start.1 = (bf16[4,640,1280]{2,1,0:T(8,128)(2,1)S(1)}, bf16[4,640,1280]{2,1,0:T(8,128)(2,1)}, u32[]{:S(2)}) copy-start(bf16[4,640,1280]{2,1,0:T(8,128)(2,1)} %w_out.1) | copy-start | bytes 19660804
  34.7 3.0 %collective-permute-start.1 = (bf16[128,640]{1,0:T(8,128)(2,1)S(1)}, bf16[128,640]{1,0:T(8,128)(2,1)S(1)}, u32[]{:S(2)}, u32[]{:S(2)}) collective-permute-start(bf16[128,640]{1,0:T(8,128)(2,1)S(1)} %reduce.1.own_ref), channel_id=1, source_target_pairs={{0,1},{1,0},{2,3},{3,2},{4,5},{5,4},{6,7},{7,6},{8,9},{9,8},{10,11... | collective-permute-start | bytes 491528 | tf_op jit(solution)/shard_map/ppermute | solution.py:251
  40.1 1.5 %collective-permute-start.2 = (bf16[128,640]{1,0:T(8,128)(2,1)S(1)}, bf16[128,640]{1,0:T(8,128)(2,1)S(1)}, u32[]{:S(2)}, u32[]{:S(2)}) collective-permute-start(bf16[128,640]{1,0:T(8,128)(2,1)S(1)} %get-tuple-element.14), channel_id=1, source_target_pairs={{0,1},{1,0},{2,3},{3,2},{4,5},{5,4},{6,7},{7,6},{8,9},{9,8},{10,11... | collective-permute-start | bytes 491528 | tf_op jit(solution)/shard_map/ppermute | solution.py:251
  59.8 3.0 %collective-permute-start.3 = (bf16[2,64,640]{2,1,0:T(8,128)(2,1)S(1)}, bf16[2,64,640]{2,1,0:T(8,128)(2,1)S(1)}, u32[]{:S(2)}, u32[]{:S(2)}) collective-permute-start(bf16[2,64,640]{2,1,0:T(8,128)(2,1)S(1)} %sum_parts.1.own_ref), channel_id=1, source_target_pairs={{0,1},{1,0},{2,3},{3,2},{4,5},{5,4},{6,7},{7,6},{8,9},{9,8},{10,11... | collective-permute-start | bytes 491528 | tf_op jit(solution)/shard_map/ppermute | solution.py:251

commit v3 on v2

v3 whole, which is shorter than its diff:
```python
import functools

import jax
import jax.numpy as jnp
import numpy as np
from jax import lax
from jax.experimental import pallas as pl
from jax.experimental.pallas import tpu as pltpu
from jax.sharding import PartitionSpec as P

F32 = jnp.float32
BF16 = jnp.bfloat16
HALF = 640
WIDE = HALF + 128
NT = (((1,), (1,)), ((), ()))


def columns(half):
    core = lax.axis_index("core")
    return pl.ds(pl.multiple_of((core if half == 0 else 1 - core) * HALF, 128), HALF)


def stats_block(peak, total):
    high = total.astype(BF16).astype(F32)
    lane = lax.broadcasted_iota(jnp.int32, (peak.shape[0], 128), 1)
    return jnp.where(lane == 0, peak, jnp.where(lane == 1, high, jnp.where(lane == 2, total - high, 0.0)))


def gather_kernel(
    pieces, tokens_hbm, slots_hbm, send_ref, stats_ref, dispatch_ref, logits_ref, tokens_ref, slots, sems
):
    clips, count, _ = tokens_ref.shape
    step = count // pieces

    def copy(b, i):
        rows = pl.ds(i * step, step)
        return pltpu.make_async_copy(tokens_hbm.at[b, rows], tokens_ref.at[b, rows], sems.at[b, i])

    slots_copy = pltpu.make_async_copy(slots_hbm, slots, sems.at[clips, 0])
    slots_copy.start()
    for b in range(clips):
        for i in range(pieces):
            copy(b, i).start()
    slots_copy.wait()
    for b in range(clips):
        for i in range(pieces):
            copy(b, i).wait()
            rows = pl.ds(i * step, step)
            logits_ref[b, :, rows] = lax.dot_general(
                slots[...], tokens_ref[b, rows, :], NT, preferred_element_type=F32
            )
    for b in range(clips):
        logits = logits_ref[b]
        peak = jnp.max(logits, axis=1, keepdims=True).astype(BF16).astype(F32)
        expd = jnp.exp(logits - peak)
        stats = stats_block(peak, jnp.sum(expd, axis=1, keepdims=True))
        dispatch_ref[b] = expd.astype(BF16)
        stats_ref[b] = stats
        send_ref[b, :, pl.ds(HALF, 128)] = stats.astype(BF16)
        send_ref[b, :, pl.ds(0, HALF)] = jnp.dot(
            dispatch_ref[b], tokens_ref[b, :, columns(1)], preferred_element_type=F32
        ).astype(BF16)


def gather(tokens, slots_t):
    clips, count, width = tokens.shape
    slots = slots_t.shape[0]
    pieces = 2
    vmem = pl.BlockSpec(memory_space=pltpu.VMEM)
    return pl.pallas_call(
        functools.partial(gather_kernel, pieces),
        out_shape=[
            pltpu.VMEM((clips, slots, WIDE), BF16),
            pltpu.VMEM((clips, slots, 128), F32),
            pltpu.VMEM((clips, slots, count), BF16),
            pltpu.VMEM((clips, slots, count), F32),
            pltpu.VMEM((clips, count, width), BF16),
        ],
        in_specs=[pl.BlockSpec(memory_space=pl.ANY)] * 2,
        out_specs=[vmem] * 5,
        scratch_shapes=[pltpu.VMEM((slots, width), BF16), pltpu.SemaphoreType.DMA((clips + 1, pieces))],
        compiler_params=pltpu.CompilerParams(vmem_limit_bytes=56 << 20),
        cost_estimate=pl.CostEstimate(
            flops=3 * clips * slots * count * width,
            bytes_accessed=2 * clips * count * width,
            transcendentals=clips * slots * count,
        ),
        name="gather",
    )(tokens, slots_t)


def keep_kernel(dispatch_ref, tokens_ref, out_ref):
    for b in range(dispatch_ref.shape[0]):
        out_ref[b] = jnp.dot(dispatch_ref[b], tokens_ref[b, :, columns(0)], preferred_element_type=F32)


def keep_half(dispatch, tokens):
    clips, slots, count = dispatch.shape
    return pl.pallas_call(
        keep_kernel,
        out_shape=pltpu.VMEM((clips, slots, HALF), F32),
        compiler_params=pltpu.CompilerParams(vmem_limit_bytes=16 << 20),
        cost_estimate=pl.CostEstimate(
            flops=2 * clips * slots * count * HALF, bytes_accessed=2 * tokens.size, transcendentals=0
        ),
        name="keep_half",
    )(dispatch, tokens)


def pack_kernel(keep_ref, stats_ref, recv_ref, out_ref):
    halves = []
    for b in range(2):
        kept, stats, got = keep_ref[b], stats_ref[b], recv_ref[b].astype(F32)
        peak_k, peak_g = stats[:, :1], got[:, HALF : HALF + 1]
        peak = jnp.maximum(peak_k, peak_g)
        scale_k, scale_g = jnp.exp(peak_k - peak), jnp.exp(peak_g - peak)
        total = scale_k * (stats[:, 1:2] + stats[:, 2:3]) + scale_g * (
            got[:, HALF + 1 : HALF + 2] + got[:, HALF + 2 : HALF + 3]
        )
        value = scale_k * kept + scale_g * got[:, :HALF]
        halves.append(jnp.concatenate([value, stats_block(peak, total)], axis=1).reshape(8, 8, WIDE))
    first, second = halves
    top = lax.broadcasted_iota(jnp.int32, first.shape, 1) < 4
    even = jnp.where(top, first, pltpu.roll(second, 4, 1)).astype(BF16)
    odd = jnp.where(top, pltpu.roll(first, 4, 1), second).astype(BF16)
    for j in range(8):
        for x in range(4):
            out_ref[8 * j + x] = even[j]
            out_ref[8 * j + 4 + x] = odd[j]


def pack(keep, stats, recv):
    return pl.pallas_call(
        pack_kernel,
        out_shape=jax.ShapeDtypeStruct((64, 8, WIDE), BF16),
        compiler_params=pltpu.CompilerParams(vmem_limit_bytes=24 << 20),
        cost_estimate=pl.CostEstimate(flops=1 << 36, bytes_accessed=100 << 20, transcendentals=0),
        name="pack",
    )(keep, stats, recv)


def reduce_kernel(parts_ref, out_ref):
    for i in range(8):
        part = parts_ref[8 * i : 8 * i + 8].astype(F32).reshape(2, 4, 8, WIDE)
        peak = part[..., HALF : HALF + 1]
        weight = jnp.exp(peak - jnp.max(peak, axis=1, keepdims=True))
        total = weight * (part[..., HALF + 1 : HALF + 2] + part[..., HALF + 2 : HALF + 3])
        weight = weight / jnp.sum(total, axis=1, keepdims=True)
        slot_in = jnp.sum(weight * part[..., :HALF], axis=1)
        out_ref[pl.ds(16 * i, 16), :] = slot_in.reshape(16, HALF).astype(BF16)


def reduce(parts):
    return pl.pallas_call(
        reduce_kernel,
        out_shape=jax.ShapeDtypeStruct((128, HALF), BF16),
        compiler_params=pltpu.CompilerParams(vmem_limit_bytes=24 << 20),
        name="reduce",
    )(parts)


def own_expert(rows, weights, lanes):
    experts = weights.shape[0]
    slot = lax.broadcasted_iota(jnp.int32, (rows.shape[0], 1), 0) % experts
    out = None
    for e in range(experts):
        here = jnp.dot(rows, weights[(e, *lanes)], preferred_element_type=F32)
        out = here if e == 0 else jnp.where(slot == e, here, out)
    return out


def first_kernel(own_ref, w_in, pre_ref):
    pre_ref[...] = own_expert(own_ref[...], w_in, (columns(0), slice(None)))


def second_kernel(pre_ref, oth_ref, w_in, w_out, hidden_ref, send_ref):
    value = pre_ref[...] + own_expert(oth_ref[...], w_in, (columns(1), slice(None)))
    hidden_ref[...] = (0.5 * value * (1.0 + lax.erf(value * np.float32(np.sqrt(0.5))))).astype(BF16)
    send_ref[...] = own_expert(hidden_ref[...], w_out, (slice(None), columns(1))).astype(BF16)


def third_kernel(hidden_ref, w_out, keep_ref):
    keep_ref[...] = own_expert(hidden_ref[...], w_out, (slice(None), columns(0)))


def stage(kernel, name, outs, *operands):
    return pl.pallas_call(
        kernel,
        out_shape=outs,
        compiler_params=pltpu.CompilerParams(vmem_limit_bytes=24 << 20),
        cost_estimate=pl.CostEstimate(
            flops=128 * sum(x.size for x in operands), bytes_accessed=2 * sum(x.size for x in operands), transcendentals=0
        ),
        name=name,
    )(*operands)


def combine_kernel(logits_ref, out_ref):
    for b in range(2):
        logits = logits_ref[b]
        expd = jnp.exp(logits - jnp.max(logits, axis=0, keepdims=True))
        combine = expd / jnp.sum(expd, axis=0, keepdims=True)
        out_ref[b] = combine.T.astype(BF16)


def combine(logits):
    clips, slots, count = logits.shape
    return pl.pallas_call(
        combine_kernel,
        out_shape=jax.ShapeDtypeStruct((clips, count, slots), BF16),
        compiler_params=pltpu.CompilerParams(vmem_limit_bytes=24 << 20),
        cost_estimate=pl.CostEstimate(flops=8 * logits.size, bytes_accessed=6 * logits.size, transcendentals=logits.size),
        name="combine",
    )(logits)


def sum_kernel(parts_ref, out_ref):
    top = lax.broadcasted_iota(jnp.int32, (2, 8, HALF), 1) < 4
    for i in range(4):
        part = parts_ref[16 * i : 16 * i + 16].astype(F32).reshape(4, 4, 8, HALF)
        part = jnp.sum(part, axis=1).reshape(2, 2, 8, HALF)
        even, odd = part[:, 0], part[:, 1]
        first = jnp.where(top, even, pltpu.roll(odd, 4, 1))
        second = jnp.where(top, pltpu.roll(even, 4, 1), odd)
        rows = pl.ds(16 * i, 16)
        out_ref[0, rows] = first.reshape(16, HALF).astype(BF16)
        out_ref[1, rows] = second.reshape(16, HALF).astype(BF16)


def sum_parts(parts):
    return pl.pallas_call(
        sum_kernel,
        out_shape=jax.ShapeDtypeStruct((2, 64, HALF), BF16),
        compiler_params=pltpu.CompilerParams(vmem_limit_bytes=24 << 20),
        name="sum_parts",
    )(parts)


def mix_own_kernel(combine_ref, own_ref, out_ref):
    for b in range(combine_ref.shape[0]):
        out_ref[b] = jnp.dot(combine_ref[b], own_ref[b], preferred_element_type=F32).astype(BF16)


def mix_kernel(pieces, combine_ref, mixed_ref, oth_ref, out_hbm, mixed, sems):
    clips, count, _ = mixed.shape
    copies = [
        pltpu.make_async_copy(mixed_ref.at[b], out_hbm.at[b, :, columns(0)], sems.at[clips, b]) for b in range(clips)
    ]
    for copy in copies:
        copy.start()
    for b in range(clips):
        for i in range(pieces):
            rows = pl.ds(i * (count // pieces), count // pieces)
            mixed[b, rows] = jnp.dot(combine_ref[b, rows], oth_ref[b], preferred_element_type=F32).astype(BF16)
            copies.append(pltpu.make_async_copy(mixed.at[b, rows], out_hbm.at[b, rows, columns(1)], sems.at[b, i]))
            copies[-1].start()
    for copy in copies:
        copy.wait()


def mix(weights, mixed, oth):
    clips, count, _ = weights.shape
    pieces = 2
    return pl.pallas_call(
        functools.partial(mix_kernel, pieces),
        out_shape=jax.ShapeDtypeStruct((clips, count, 2 * HALF), BF16),
        in_specs=[pl.BlockSpec(memory_space=pltpu.VMEM)] * 3,
        out_specs=pl.BlockSpec(memory_space=pl.ANY),
        scratch_shapes=[pltpu.VMEM((clips, count, HALF), BF16), pltpu.SemaphoreType.DMA((clips + 1, pieces))],
        compiler_params=pltpu.CompilerParams(vmem_limit_bytes=32 << 20),
        name="mix",
    )(weights, mixed, oth)


def swap(x):
    return lax.ppermute(x, "core", [(0, 1), (1, 0)])


def exchange(x):
    return lax.all_to_all(x, ("dp", "x"), 0, 0, tiled=True)


def on_device(tokens, slot_param, w_in, w_out):
    send, stats, dispatch, logits, held = gather(
        pltpu.with_memory_space_constraint(tokens, pltpu.HBM),
        pltpu.with_memory_space_constraint(slot_param.T, pltpu.HBM),
    )
    keep, weights = lax.optimization_barrier((keep_half(dispatch, held), combine(logits)))
    own = reduce(exchange(pack(keep, stats, swap(send))))
    pre = stage(first_kernel, "first", pltpu.VMEM((128, HALF), F32), own, w_in)
    outs = [pltpu.VMEM((128, HALF), BF16)] * 2
    hidden, send = stage(second_kernel, "second", outs, pre, swap(own), w_in, w_out)
    keep = stage(third_kernel, "third", pltpu.VMEM((128, HALF), F32), hidden, w_out)
    summed = (keep + swap(send).astype(F32)).astype(BF16).reshape(16, 1, 8, HALF)
    own = sum_parts(exchange(jnp.broadcast_to(summed, (16, 4, 8, HALF)).reshape(64, 8, HALF)))
    mixed = stage(mix_own_kernel, "mix_own", pltpu.VMEM(weights.shape[:2] + (HALF,), BF16), weights, own)
    return mix(weights, mixed, swap(own))


def solution(mesh):
    ctx = ("x", "core")
    split = jax.sharding.Mesh(np.asarray(mesh.devices).reshape(16, 4, 2), ("dp",) + ctx)
    placed = (P("dp", ctx, None), P(), P("dp", None, ctx), P("dp", ctx, None))
    return jax.shard_map(
        on_device, mesh=split, in_specs=placed, out_specs=P("dp", ctx, None), check_vma=False
    )
```

time: 66.5 us -> 63.5 us (0.955)
  waiting for transfers between devices: 3.87 us -> 0.81 us
    ppermute x4, waiting for transfers between devices: 3.87 us -> 0.81 us  [swap(): return lax.ppermute(x, 'core', [(0, 1), (1, 0)])]
    pallas_call x2 -> x6, Pallas kernels: 5.91 us -> 6.92 us  [the longest x4 3.92 us: stage(): pl.pallas_call(kernel, out_shape=outs, compiler_params=pltpu.CompilerPara...]
    pallas_call x1, Pallas kernels: 4.97 us -> 3.99 us  [gather(): pl.pallas_call(functools.partial(gather_kernel, pieces), out_shape=[pltpu...]
  transfers between devices with their start and end apart: 4 -> 4, of which waited for: 4 -> 4; matrix products, arithmetic and copies ran while one was open for 0% -> 0% of each run, Pallas kernels for 0% -> 5%
where the time goes in v3:
time: 63.5 us; the launch traced here: 63.4 us
  blocking collectives  44.5 us (70%)
  Pallas kernels  12 us (19%)
  starting transfers between devices  5.9 us (9%)
  waiting for transfers between devices  0.81 us (1%)
    all_to_all x2, blocking collectives, exchange(): return lax.all_to_all(x, ('dp', 'x'), 0, 0, tiled=True)  44.5 us
    ppermute x4, starting transfers between devices, swap(): return lax.ppermute(x, 'core', [(0, 1), (1, 0)])  5.9 us
    pallas_call x1, Pallas kernels, gather(): pl.pallas_call(functools.partial(gather_kernel, pieces), out_shape=[pltpu...  3.99 us
    pallas_call x4, Pallas kernels, stage(): pl.pallas_call(kernel, out_shape=outs, compiler_params=pltpu.CompilerPara...  3.92 us
    pallas_call x1, Pallas kernels, mix(): pl.pallas_call(functools.partial(mix_kernel, pieces), out_shape=jax.Shape...  2.41 us
  transfers between devices with their start and end apart: 4, of which 4 were waited for; matrix products, arithmetic and copies ran while one was open for 0% of the time, Pallas kernels for 5%

profile of v3, /device:TPU:1, one launch (start us, length us, event | category | flops | bytes accessed | tf_op | source)
XLA Modules:
  0.0 63.4 jit_solution(7468696473191241373)
XLA Ops:
  0.0 4.0 %gather.1 = (bf16[2,64,768]{2,1,0:T(8,128)(2,1)S(1)}, f32[2,64,128]{2,1,0:T(8,128)S(1)}, bf16[2,64,1024]{2,1,0:T(8,128)(2,1)S(1)}, f32[2,64,1024]{2,1,0:T(8,128)S(1)}, bf16[2,1024,1280]{2,1,0:T(8,128)(2,1)S(1)}) custom-call(bf16[2,1024,1280]{2,1,0:T(8,128)(2,1)} %tokens_hbm.1, bf16[64,1280]{1,0:T(8,128)(2,1)} %bitcast.9), custom_call_target="tpu_custom_call" | custom-call | flops 503316480 | bytes 5242880 | tf_op jit(solution)/shard_map/gather/pallas_call | solution.py:70
  4.0 1.5 %collective-permute-start = (bf16[2,64,768]{2,1,0:T(8,128)(2,1)S(1)}, bf16[2,64,768]{2,1,0:T(8,128)(2,1)S(1)}, u32[]{:S(2)}, u32[]{:S(2)}) collective-permute-start(bf16[2,64,768]{2,1,0:T(8,128)(2,1)S(1)} %get-tuple-element.20), channel_id=1, source_target_pairs={{0,1},{1,0},{2,3},{3,2},{4,5},{5,4},{6,7},{7,6},{8,9},{9,8},{10,11... | collective-permute-start | bytes 589832 | tf_op jit(solution)/shard_map/ppermute | solution.py:276
  5.5 0.3 combine.1.combine_ref
  5.8 0.0 slice-start
  5.8 0.6 keep_half.1.keep_ref
  6.4 0.2 collective-permute-done.recv_ref
  6.6 0.0 slice-start.2
  6.6 0.0 slice-start.1
  6.6 0.0 slice-start.3
  6.6 0.3 pack.1
  6.9 26.5 %all_to_all.10.parts_ref = bf16[64,8,768]{2,1,0:T(8,128)(2,1)S(1)} all-to-all(bf16[64,8,768]{2,1,0:T(8,128)(2,1)S(1)} %pack.1), channel_id=1, replica_groups=mesh['dp'=16,'x'=4,'core'=2] {'dp','x'}, dimensions={0} | all-to-all | bytes 1572864 | tf_op jit(solution)/shard_map/all_to_all | solution.py:280
  33.4 0.4 reduce.1.own_ref
  33.8 2.0 %collective-permute-start.1 = (bf16[128,640]{1,0:T(8,128)(2,1)S(1)}, bf16[128,640]{1,0:T(8,128)(2,1)S(1)}, u32[]{:S(2)}, u32[]{:S(2)}) collective-permute-start(bf16[128,640]{1,0:T(8,128)(2,1)S(1)} %reduce.1.own_ref), channel_id=1, source_target_pairs={{0,1},{1,0},{2,3},{3,2},{4,5},{5,4},{6,7},{7,6},{8,9},{9,8},{10,11... | collective-permute-start | bytes 491528 | tf_op jit(solution)/shard_map/ppermute | solution.py:276
  35.8 0.0 slice-done
  35.8 0.0 slice-done.1
  35.8 0.8 %first.1.pre_ref = f32[128,640]{1,0:T(8,128)S(1)} custom-call(bf16[128,640]{1,0:T(8,128)(2,1)S(1)} %reduce.1.own_ref, bf16[4,1280,640]{2,1,0:T(8,128)(2,1)S(1)} %bitcast.5), custom_call_target="tpu_custom_call" | custom-call | flops 429916160 | bytes 6717440 | tf_op jit(solution)/shard_map/first/pallas_call | solution.py:187
  36.6 0.2 collective-permute-done.1.oth_ref
  36.8 0.0 slice-done.2
  36.8 0.0 slice-done.3
  36.8 1.5 %second.1 = (bf16[128,640]{1,0:T(8,128)(2,1)S(1)}, bf16[128,640]{1,0:T(8,128)(2,1)S(1)}) custom-call(f32[128,640]{1,0:T(8,128)S(1)} %first.1.pre_ref, bf16[128,640]{1,0:T(8,128)(2,1)S(1)} %collective-permute-done.1.oth_ref, bf16[4,1280,640]{2,1,0:T(8,128)(2,1)S(1)} %bitcast.5, bf16[4,640,1280]{2,1,0:T(8,128)(2,1)S(1)} %bitcast.7), custom_call_target="tpu_custom_call" | custom-call | flops 859832320 | bytes 13434880 | tf_op jit(solution)/shard_map/second/pallas_call | solution.py:187
  38.3 0.5 collective-permute-start.2
  38.8 0.8 %third.1 = f32[128,640]{1,0:T(8,128)S(1)} custom-call(bf16[128,640]{1,0:T(8,128)(2,1)S(1)} %get-tuple-element.21.hidden_ref, bf16[4,640,1280]{2,1,0:T(8,128)(2,1)S(1)} %bitcast.7), custom_call_target="tpu_custom_call" | custom-call | flops 429916160 | bytes 6717440 | tf_op jit(solution)/shard_map/third/pallas_call | solution.py:187
  39.6 0.2 collective-permute-done.2
  39.9 0.1 broadcast_in_dim.8
  39.9 18.0 %all_to_all.11.parts_ref = bf16[64,8,640]{2,1,0:T(8,128)(2,1)S(1)} all-to-all(bf16[64,8,640]{2,1,0:T(8,128)(2,1)S(1)} %bitcast.8), channel_id=1, replica_groups=mesh['dp'=16,'x'=4,'core'=2] {'dp','x'}, dimensions={0} | all-to-all | bytes 1310720 | tf_op jit(solution)/shard_map/all_to_all | solution.py:280
  57.9 0.1 sum_parts.1.own_ref
  58.0 1.9 %collective-permute-start.3 = (bf16[2,64,640]{2,1,0:T(8,128)(2,1)S(1)}, bf16[2,64,640]{2,1,0:T(8,128)(2,1)S(1)}, u32[]{:S(2)}, u32[]{:S(2)}) collective-permute-start(bf16[2,64,640]{2,1,0:T(8,128)(2,1)S(1)} %sum_parts.1.own_ref), channel_id=1, source_target_pairs={{0,1},{1,0},{2,3},{3,2},{4,5},{5,4},{6,7},{7,6},{8,9},{9,8},{10,11... | collective-permute-start | bytes 491528 | tf_op jit(solution)/shard_map/ppermute | solution.py:276
  60.0 0.8 %mix_own.1.mixed_ref = bf16[2,1024,640]{2,1,0:T(8,128)(2,1)S(1)} custom-call(bf16[2,1024,64]{2,1,0:T(8,128)(2,1)S(1)} %combine.1.combine_ref, bf16[2,64,640]{2,1,0:T(8,128)(2,1)S(1)} %sum_parts.1.own_ref), custom_call_target="tpu_custom_call" | custom-call | flops 27262976 | bytes 425984 | tf_op jit(solution)/shard_map/mix_own/pallas_call | solution.py:187
  60.8 0.2 collective-permute-done.3.oth_ref
  61.0 2.4 %mix.1 = bf16[2,1024,1280]{2,1,0:T(8,128)(2,1)} custom-call(bf16[2,1024,64]{2,1,0:T(8,128)(2,1)S(1)} %combine.1.combine_ref, bf16[2,1024,640]{2,1,0:T(8,128)(2,1)S(1)} %mix_own.1.mixed_ref, bf16[2,64,640]{2,1,0:T(8,128)(2,1)S(1)} %collective-permute-done.3.oth_ref), custom_call_target="tpu_custom_call" | custom-call | tf_op jit(solution)/shard_map/mix/pallas_call | solution.py:264
  (3 shorter events, 0.0 us)
Async XLA Ops:
  4.0 2.6 %collective-permute-start = (bf16[2,64,768]{2,1,0:T(8,128)(2,1)S(1)}, bf16[2,64,768]{2,1,0:T(8,128)(2,1)S(1)}, u32[]{:S(2)}, u32[]{:S(2)}) collective-permute-start(bf16[2,64,768]{2,1,0:T(8,128)(2,1)S(1)} %get-tuple-element.20), channel_id=1, source_target_pairs={{0,1},{1,0},{2,3},{3,2},{4,5},{5,4},{6,7},{7,6},{8,9},{9,8},{10,11... | collective-permute-start | bytes 589832 | tf_op jit(solution)/shard_map/ppermute | solution.py:276
  5.8 30.0 %slice-start = ((s8[6553600]{0:T(1024)(128)(4,1)}), s8[4194304]{0:T(1024)(128)(4,1)S(1)}, s32[]{:S(2)}) async-start(s8[6553600]{0:T(1024)(128)(4,1)} %bitcast.4), calls=%async_computation.2 | async-start | bytes 8388608
  6.6 30.2 %slice-start.2 = ((s8[6553600]{0:T(1024)(128)(4,1)}), s8[4194304]{0:T(1024)(128)(4,1)S(1)}, s32[]{:S(2)}) async-start(s8[6553600]{0:T(1024)(128)(4,1)} %bitcast.6), calls=%async_computation.4 | async-start | bytes 8388608
  6.6 29.2 %slice-start.1 = ((s8[6553600]{0:T(1024)(128)(4,1)}), s8[2359296]{0:T(1024)(128)(4,1)S(1)}, s32[]{:S(2)}) async-start(s8[6553600]{0:T(1024)(128)(4,1)} %bitcast.4), calls=%async_computation.3 | async-start | bytes 4718592
  6.6 30.2 %slice-start.3 = ((s8[6553600]{0:T(1024)(128)(4,1)}), s8[2359296]{0:T(1024)(128)(4,1)S(1)}, s32[]{:S(2)}) async-start(s8[6553600]{0:T(1024)(128)(4,1)} %bitcast.6), calls=%async_computation.5 | async-start | bytes 4718592
  33.8 3.0 %collective-permute-start.1 = (bf16[128,640]{1,0:T(8,128)(2,1)S(1)}, bf16[128,640]{1,0:T(8,128)(2,1)S(1)}, u32[]{:S(2)}, u32[]{:S(2)}) collective-permute-start(bf16[128,640]{1,0:T(8,128)(2,1)S(1)} %reduce.1.own_ref), channel_id=1, source_target_pairs={{0,1},{1,0},{2,3},{3,2},{4,5},{5,4},{6,7},{7,6},{8,9},{9,8},{10,11... | collective-permute-start | bytes 491528 | tf_op jit(solution)/shard_map/ppermute | solution.py:276
  38.3 1.5 %collective-permute-start.2 = (bf16[128,640]{1,0:T(8,128)(2,1)S(1)}, bf16[128,640]{1,0:T(8,128)(2,1)S(1)}, u32[]{:S(2)}, u32[]{:S(2)}) collective-permute-start(bf16[128,640]{1,0:T(8,128)(2,1)S(1)} %get-tuple-element.22), channel_id=1, source_target_pairs={{0,1},{1,0},{2,3},{3,2},{4,5},{5,4},{6,7},{7,6},{8,9},{9,8},{10,11... | collective-permute-start | bytes 491528 | tf_op jit(solution)/shard_map/ppermute | solution.py:276
  58.0 3.0 %collective-permute-start.3 = (bf16[2,64,640]{2,1,0:T(8,128)(2,1)S(1)}, bf16[2,64,640]{2,1,0:T(8,128)(2,1)S(1)}, u32[]{:S(2)}, u32[]{:S(2)}) collective-permute-start(bf16[2,64,640]{2,1,0:T(8,128)(2,1)S(1)} %sum_parts.1.own_ref), channel_id=1, source_target_pairs={{0,1},{1,0},{2,3},{3,2},{4,5},{5,4},{6,7},{7,6},{8,9},{9,8},{10,11... | collective-permute-start | bytes 491528 | tf_op jit(solution)/shard_map/ppermute | solution.py:276

commit v4 on v3

--- a/solution.py
+++ b/solution.py
@@ -140,14 +140,15 @@
 
 
 def reduce_kernel(parts_ref, out_ref):
+    stats = parts_ref[:, :, pl.ds(HALF, 128)].astype(F32).reshape(16, 4, 8, 128)
+    peak = stats[..., :1]
+    weight = jnp.exp(peak - jnp.max(peak, axis=1, keepdims=True))
+    total = jnp.sum(weight * (stats[..., 1:2] + stats[..., 2:3]), axis=1, keepdims=True)
+    weight = jnp.broadcast_to(weight / total, (16, 4, 8, 128))
     for i in range(8):
-        part = parts_ref[8 * i : 8 * i + 8].astype(F32).reshape(2, 4, 8, WIDE)
-        peak = part[..., HALF : HALF + 1]
-        weight = jnp.exp(peak - jnp.max(peak, axis=1, keepdims=True))
-        total = weight * (part[..., HALF + 1 : HALF + 2] + part[..., HALF + 2 : HALF + 3])
-        weight = weight / jnp.sum(total, axis=1, keepdims=True)
-        slot_in = jnp.sum(weight * part[..., :HALF], axis=1)
-        out_ref[pl.ds(16 * i, 16), :] = slot_in.reshape(16, HALF).astype(BF16)
+        scale = jnp.concatenate([weight[2 * i : 2 * i + 2]] * (HALF // 128), axis=-1)
+        part = parts_ref[8 * i : 8 * i + 8, :, pl.ds(0, HALF)].astype(F32).reshape(2, 4, 8, HALF)
+        out_ref[pl.ds(16 * i, 16), :] = jnp.sum(scale * part, axis=1).reshape(16, HALF).astype(BF16)
 
 
 def reduce(parts):
@@ -163,9 +164,11 @@
     experts = weights.shape[0]
     slot = lax.broadcasted_iota(jnp.int32, (rows.shape[0], 1), 0) % experts
     out = None
-    for e in range(experts):
-        here = jnp.dot(rows, weights[(e, *lanes)], preferred_element_type=F32)
-        out = here if e == 0 else jnp.where(slot == e, here, out)
+    for e in range(0, experts, 2):
+        pair = jnp.concatenate([weights[(e, *lanes)], weights[(e + 1, *lanes)]], axis=1)
+        here = jnp.dot(rows, pair, preferred_element_type=F32)
+        here = jnp.where(slot % 2 == 0, here[:, :HALF], here[:, HALF:])
+        out = here if e == 0 else jnp.where(slot >= e, here, out)
     return out
 
 

time: 63.5 us -> 63.4 us (level)
  no operation moved by 1% of the time
where the time goes in v4:
time: 63.4 us; the launch traced here: 63.2 us
  blocking collectives  44.5 us (70%)
  Pallas kernels  11.6 us (18%)
  starting transfers between devices  5.88 us (9%)
  waiting for transfers between devices  1.05 us (2%)
    all_to_all x2, blocking collectives, exchange(): return lax.all_to_all(x, ('dp', 'x'), 0, 0, tiled=True)  44.5 us
    ppermute x4, starting transfers between devices, swap(): return lax.ppermute(x, 'core', [(0, 1), (1, 0)])  5.88 us
    pallas_call x1, Pallas kernels, gather(): pl.pallas_call(functools.partial(gather_kernel, pieces), out_shape=[pltpu...  3.99 us
    pallas_call x4, Pallas kernels, stage(): pl.pallas_call(kernel, out_shape=outs, compiler_params=pltpu.CompilerPara...  3.56 us
    pallas_call x1, Pallas kernels, mix(): pl.pallas_call(functools.partial(mix_kernel, pieces), out_shape=jax.Shape...  2.41 us
  transfers between devices with their start and end apart: 4, of which 4 were waited for; matrix products, arithmetic and copies ran while one was open for 0% of the time, Pallas kernels for 5%

profile of v4, /device:TPU:1, one launch (start us, length us, event | category | flops | bytes accessed | tf_op | source)
XLA Modules:
  0.0 63.2 jit_solution(16211303604591810524)
XLA Ops:
  0.0 4.0 %gather.1 = (bf16[2,64,768]{2,1,0:T(8,128)(2,1)S(1)}, f32[2,64,128]{2,1,0:T(8,128)S(1)}, bf16[2,64,1024]{2,1,0:T(8,128)(2,1)S(1)}, f32[2,64,1024]{2,1,0:T(8,128)S(1)}, bf16[2,1024,1280]{2,1,0:T(8,128)(2,1)S(1)}) custom-call(bf16[2,1024,1280]{2,1,0:T(8,128)(2,1)} %tokens_hbm.1, bf16[64,1280]{1,0:T(8,128)(2,1)} %bitcast.9), custom_call_target="tpu_custom_call" | custom-call | flops 503316480 | bytes 5242880 | tf_op jit(solution)/shard_map/gather/pallas_call | solution.py:70
  4.0 1.5 %collective-permute-start = (bf16[2,64,768]{2,1,0:T(8,128)(2,1)S(1)}, bf16[2,64,768]{2,1,0:T(8,128)(2,1)S(1)}, u32[]{:S(2)}, u32[]{:S(2)}) collective-permute-start(bf16[2,64,768]{2,1,0:T(8,128)(2,1)S(1)} %get-tuple-element.20), channel_id=1, source_target_pairs={{0,1},{1,0},{2,3},{3,2},{4,5},{5,4},{6,7},{7,6},{8,9},{9,8},{10,11... | collective-permute-start | bytes 589832 | tf_op jit(solution)/shard_map/ppermute | solution.py:279
  5.5 0.3 combine.1.combine_ref
  5.8 0.0 slice-start
  5.8 0.6 keep_half.1.keep_ref
  6.4 0.2 collective-permute-done.recv_ref
  6.6 0.0 slice-start.2
  6.6 0.0 slice-start.1
  6.6 0.0 slice-start.3
  6.6 0.3 pack.1
  6.9 26.5 %all_to_all.10.parts_ref = bf16[64,8,768]{2,1,0:T(8,128)(2,1)S(1)} all-to-all(bf16[64,8,768]{2,1,0:T(8,128)(2,1)S(1)} %pack.1), channel_id=1, replica_groups=mesh['dp'=16,'x'=4,'core'=2] {'dp','x'}, dimensions={0} | all-to-all | bytes 1572864 | tf_op jit(solution)/shard_map/all_to_all | solution.py:283
  33.4 0.3 reduce.1.own_ref
  33.8 2.0 %collective-permute-start.1 = (bf16[128,640]{1,0:T(8,128)(2,1)S(1)}, bf16[128,640]{1,0:T(8,128)(2,1)S(1)}, u32[]{:S(2)}, u32[]{:S(2)}) collective-permute-start(bf16[128,640]{1,0:T(8,128)(2,1)S(1)} %reduce.1.own_ref), channel_id=1, source_target_pairs={{0,1},{1,0},{2,3},{3,2},{4,5},{5,4},{6,7},{7,6},{8,9},{9,8},{10,11... | collective-permute-start | bytes 491528 | tf_op jit(solution)/shard_map/ppermute | solution.py:279
  35.7 0.0 slice-done
  35.7 0.0 slice-done.1
  35.7 0.7 %first.1.pre_ref = f32[128,640]{1,0:T(8,128)S(1)} custom-call(bf16[128,640]{1,0:T(8,128)(2,1)S(1)} %reduce.1.own_ref, bf16[4,1280,640]{2,1,0:T(8,128)(2,1)S(1)} %bitcast.5), custom_call_target="tpu_custom_call" | custom-call | flops 429916160 | bytes 6717440 | tf_op jit(solution)/shard_map/first/pallas_call | solution.py:190
  36.4 0.3 collective-permute-done.1.oth_ref
  36.8 0.0 slice-done.2
  36.8 0.0 slice-done.3
  36.8 1.4 %second.1 = (bf16[128,640]{1,0:T(8,128)(2,1)S(1)}, bf16[128,640]{1,0:T(8,128)(2,1)S(1)}) custom-call(f32[128,640]{1,0:T(8,128)S(1)} %first.1.pre_ref, bf16[128,640]{1,0:T(8,128)(2,1)S(1)} %collective-permute-done.1.oth_ref, bf16[4,1280,640]{2,1,0:T(8,128)(2,1)S(1)} %bitcast.5, bf16[4,640,1280]{2,1,0:T(8,128)(2,1)S(1)} %bitcast.7), custom_call_target="tpu_custom_call" | custom-call | flops 859832320 | bytes 13434880 | tf_op jit(solution)/shard_map/second/pallas_call | solution.py:190
  38.2 0.5 collective-permute-start.2
  38.6 0.7 %third.1 = f32[128,640]{1,0:T(8,128)S(1)} custom-call(bf16[128,640]{1,0:T(8,128)(2,1)S(1)} %get-tuple-element.21.hidden_ref, bf16[4,640,1280]{2,1,0:T(8,128)(2,1)S(1)} %bitcast.7), custom_call_target="tpu_custom_call" | custom-call | flops 429916160 | bytes 6717440 | tf_op jit(solution)/shard_map/third/pallas_call | solution.py:190
  39.3 0.3 collective-permute-done.2
  39.7 0.1 broadcast_in_dim.8
  39.8 18.0 %all_to_all.11.parts_ref = bf16[64,8,640]{2,1,0:T(8,128)(2,1)S(1)} all-to-all(bf16[64,8,640]{2,1,0:T(8,128)(2,1)S(1)} %bitcast.8), channel_id=1, replica_groups=mesh['dp'=16,'x'=4,'core'=2] {'dp','x'}, dimensions={0} | all-to-all | bytes 1310720 | tf_op jit(solution)/shard_map/all_to_all | solution.py:283
  57.7 0.1 sum_parts.1.own_ref
  57.9 1.9 %collective-permute-start.3 = (bf16[2,64,640]{2,1,0:T(8,128)(2,1)S(1)}, bf16[2,64,640]{2,1,0:T(8,128)(2,1)S(1)}, u32[]{:S(2)}, u32[]{:S(2)}) collective-permute-start(bf16[2,64,640]{2,1,0:T(8,128)(2,1)S(1)} %sum_parts.1.own_ref), channel_id=1, source_target_pairs={{0,1},{1,0},{2,3},{3,2},{4,5},{5,4},{6,7},{7,6},{8,9},{9,8},{10,11... | collective-permute-start | bytes 491528 | tf_op jit(solution)/shard_map/ppermute | solution.py:279
  59.8 0.8 %mix_own.1.mixed_ref = bf16[2,1024,640]{2,1,0:T(8,128)(2,1)S(1)} custom-call(bf16[2,1024,64]{2,1,0:T(8,128)(2,1)S(1)} %combine.1.combine_ref, bf16[2,64,640]{2,1,0:T(8,128)(2,1)S(1)} %sum_parts.1.own_ref), custom_call_target="tpu_custom_call" | custom-call | flops 27262976 | bytes 425984 | tf_op jit(solution)/shard_map/mix_own/pallas_call | solution.py:190
  60.6 0.2 collective-permute-done.3.oth_ref
  60.8 2.4 %mix.1 = bf16[2,1024,1280]{2,1,0:T(8,128)(2,1)} custom-call(bf16[2,1024,64]{2,1,0:T(8,128)(2,1)S(1)} %combine.1.combine_ref, bf16[2,1024,640]{2,1,0:T(8,128)(2,1)S(1)} %mix_own.1.mixed_ref, bf16[2,64,640]{2,1,0:T(8,128)(2,1)S(1)} %collective-permute-done.3.oth_ref), custom_call_target="tpu_custom_call" | custom-call | tf_op jit(solution)/shard_map/mix/pallas_call | solution.py:267
  (3 shorter events, 0.0 us)
Async XLA Ops:
  4.0 2.6 %collective-permute-start = (bf16[2,64,768]{2,1,0:T(8,128)(2,1)S(1)}, bf16[2,64,768]{2,1,0:T(8,128)(2,1)S(1)}, u32[]{:S(2)}, u32[]{:S(2)}) collective-permute-start(bf16[2,64,768]{2,1,0:T(8,128)(2,1)S(1)} %get-tuple-element.20), channel_id=1, source_target_pairs={{0,1},{1,0},{2,3},{3,2},{4,5},{5,4},{6,7},{7,6},{8,9},{9,8},{10,11... | collective-permute-start | bytes 589832 | tf_op jit(solution)/shard_map/ppermute | solution.py:279
  5.8 30.0 %slice-start = ((s8[6553600]{0:T(1024)(128)(4,1)}), s8[4194304]{0:T(1024)(128)(4,1)S(1)}, s32[]{:S(2)}) async-start(s8[6553600]{0:T(1024)(128)(4,1)} %bitcast.4), calls=%async_computation.2 | async-start | bytes 8388608
  6.6 30.2 %slice-start.2 = ((s8[6553600]{0:T(1024)(128)(4,1)}), s8[4194304]{0:T(1024)(128)(4,1)S(1)}, s32[]{:S(2)}) async-start(s8[6553600]{0:T(1024)(128)(4,1)} %bitcast.6), calls=%async_computation.4 | async-start | bytes 8388608
  6.6 29.2 %slice-start.1 = ((s8[6553600]{0:T(1024)(128)(4,1)}), s8[2359296]{0:T(1024)(128)(4,1)S(1)}, s32[]{:S(2)}) async-start(s8[6553600]{0:T(1024)(128)(4,1)} %bitcast.4), calls=%async_computation.3 | async-start | bytes 4718592
  6.6 30.2 %slice-start.3 = ((s8[6553600]{0:T(1024)(128)(4,1)}), s8[2359296]{0:T(1024)(128)(4,1)S(1)}, s32[]{:S(2)}) async-start(s8[6553600]{0:T(1024)(128)(4,1)} %bitcast.6), calls=%async_computation.5 | async-start | bytes 4718592
  33.8 3.0 %collective-permute-start.1 = (bf16[128,640]{1,0:T(8,128)(2,1)S(1)}, bf16[128,640]{1,0:T(8,128)(2,1)S(1)}, u32[]{:S(2)}, u32[]{:S(2)}) collective-permute-start(bf16[128,640]{1,0:T(8,128)(2,1)S(1)} %reduce.1.own_ref), channel_id=1, source_target_pairs={{0,1},{1,0},{2,3},{3,2},{4,5},{5,4},{6,7},{7,6},{8,9},{9,8},{10,11... | collective-permute-start | bytes 491528 | tf_op jit(solution)/shard_map/ppermute | solution.py:279
  38.2 1.5 %collective-permute-start.2 = (bf16[128,640]{1,0:T(8,128)(2,1)S(1)}, bf16[128,640]{1,0:T(8,128)(2,1)S(1)}, u32[]{:S(2)}, u32[]{:S(2)}) collective-permute-start(bf16[128,640]{1,0:T(8,128)(2,1)S(1)} %get-tuple-element.22), channel_id=1, source_target_pairs={{0,1},{1,0},{2,3},{3,2},{4,5},{5,4},{6,7},{7,6},{8,9},{9,8},{10,11... | collective-permute-start | bytes 491528 | tf_op jit(solution)/shard_map/ppermute | solution.py:279
  57.9 3.0 %collective-permute-start.3 = (bf16[2,64,640]{2,1,0:T(8,128)(2,1)S(1)}, bf16[2,64,640]{2,1,0:T(8,128)(2,1)S(1)}, u32[]{:S(2)}, u32[]{:S(2)}) collective-permute-start(bf16[2,64,640]{2,1,0:T(8,128)(2,1)S(1)} %sum_parts.1.own_ref), channel_id=1, source_target_pairs={{0,1},{1,0},{2,3},{3,2},{4,5},{5,4},{6,7},{7,6},{8,9},{9,8},{10,11... | collective-permute-start | bytes 491528 | tf_op jit(solution)/shard_map/ppermute | solution.py:279

commit v5 on v4

--- a/solution.py
+++ b/solution.py
@@ -12,6 +12,7 @@
 BF16 = jnp.bfloat16
 HALF = 640
 WIDE = HALF + 128
+EARLY = 256
 NT = (((1,), (1,)), ((), ()))
 
 
@@ -218,16 +219,12 @@
 
 
 def sum_kernel(parts_ref, out_ref):
-    top = lax.broadcasted_iota(jnp.int32, (2, 8, HALF), 1) < 4
-    for i in range(4):
-        part = parts_ref[16 * i : 16 * i + 16].astype(F32).reshape(4, 4, 8, HALF)
-        part = jnp.sum(part, axis=1).reshape(2, 2, 8, HALF)
-        even, odd = part[:, 0], part[:, 1]
-        first = jnp.where(top, even, pltpu.roll(odd, 4, 1))
-        second = jnp.where(top, pltpu.roll(even, 4, 1), odd)
-        rows = pl.ds(16 * i, 16)
-        out_ref[0, rows] = first.reshape(16, HALF).astype(BF16)
-        out_ref[1, rows] = second.reshape(16, HALF).astype(BF16)
+    row = lax.broadcasted_iota(jnp.int32, (128, 512), 0)
+    part = lax.broadcasted_iota(jnp.int32, (128, 512), 1)
+    same = ((row // 64) * 4 + row % 4 == part % 8) & ((row % 64) // 4 == part // 32)
+    ones = jnp.where(same, 1.0, 0.0).astype(BF16)
+    total = jnp.dot(ones, parts_ref[...].reshape(512, HALF), preferred_element_type=F32)
+    out_ref[...] = total.astype(BF16).reshape(2, 64, HALF)
 
 
 def sum_parts(parts):
@@ -239,18 +236,47 @@
     )(parts)
 
 
-def mix_own_kernel(combine_ref, own_ref, out_ref):
-    for b in range(combine_ref.shape[0]):
-        out_ref[b] = jnp.dot(combine_ref[b], own_ref[b], preferred_element_type=F32).astype(BF16)
-
-
-def mix_kernel(pieces, combine_ref, mixed_ref, oth_ref, out_hbm, mixed, sems):
+def mix_own_kernel(early, combine_ref, own_ref, out_hbm, held_ref, sem):
+    clips, count, _ = held_ref.shape
+    rows = pl.ds(0, early)
+    held_ref[0, rows] = jnp.dot(combine_ref[0, rows], own_ref[0], preferred_element_type=F32).astype(BF16)
+    copy = pltpu.make_async_copy(held_ref.at[0, rows], out_hbm.at[0, rows, columns(0)], sem)
+    copy.start()
+    rows = pl.ds(early, count - early)
+    held_ref[0, rows] = jnp.dot(combine_ref[0, rows], own_ref[0], preferred_element_type=F32).astype(BF16)
+    for b in range(1, clips):
+        held_ref[b] = jnp.dot(combine_ref[b], own_ref[b], preferred_element_type=F32).astype(BF16)
+    copy.wait()
+
+
+def mix_own(weights, own):
+    clips, count, _ = weights.shape
+    vmem = pl.BlockSpec(memory_space=pltpu.VMEM)
+    return pl.pallas_call(
+        functools.partial(mix_own_kernel, EARLY),
+        out_shape=[
+            jax.ShapeDtypeStruct((clips, count, 2 * HALF), BF16),
+            pltpu.VMEM((clips, count, HALF), BF16),
+        ],
+        in_specs=[vmem] * 2,
+        out_specs=[pl.BlockSpec(memory_space=pl.ANY), vmem],
+        scratch_shapes=[pltpu.SemaphoreType.DMA(())],
+        compiler_params=pltpu.CompilerParams(vmem_limit_bytes=24 << 20),
+        cost_estimate=pl.CostEstimate(
+            flops=2 * weights.size * HALF, bytes_accessed=2 * clips * count * HALF, transcendentals=0
+        ),
+        name="mix_own",
+    )(weights, own)
+
+
+def mix_kernel(pieces, early, combine_ref, oth_ref, held_ref, _, out_hbm, mixed, sems):
     clips, count, _ = mixed.shape
-    copies = [
-        pltpu.make_async_copy(mixed_ref.at[b], out_hbm.at[b, :, columns(0)], sems.at[clips, b]) for b in range(clips)
-    ]
-    for copy in copies:
-        copy.start()
+    copies = []
+    for b in range(clips):
+        first = early if b == 0 else 0
+        rows = pl.ds(first, count - first)
+        copies.append(pltpu.make_async_copy(held_ref.at[b, rows], out_hbm.at[b, rows, columns(0)], sems.at[clips, b]))
+        copies[-1].start()
     for b in range(clips):
         for i in range(pieces):
             rows = pl.ds(i * (count // pieces), count // pieces)
@@ -261,18 +287,20 @@
         copy.wait()
 
 
-def mix(weights, mixed, oth):
+def mix(weights, oth, held, out):
     clips, count, _ = weights.shape
     pieces = 2
-    return pl.pallas_call(
-        functools.partial(mix_kernel, pieces),
-        out_shape=jax.ShapeDtypeStruct((clips, count, 2 * HALF), BF16),
-        in_specs=[pl.BlockSpec(memory_space=pltpu.VMEM)] * 3,
-        out_specs=pl.BlockSpec(memory_space=pl.ANY),
+    vmem, hbm = pl.BlockSpec(memory_space=pltpu.VMEM), pl.BlockSpec(memory_space=pl.ANY)
+    return pl.pallas_call(
+        functools.partial(mix_kernel, pieces, EARLY),
+        out_shape=jax.ShapeDtypeStruct(out.shape, BF16),
+        in_specs=[vmem] * 3 + [hbm],
+        out_specs=hbm,
         scratch_shapes=[pltpu.VMEM((clips, count, HALF), BF16), pltpu.SemaphoreType.DMA((clips + 1, pieces))],
+        input_output_aliases={3: 0},
         compiler_params=pltpu.CompilerParams(vmem_limit_bytes=32 << 20),
         name="mix",
-    )(weights, mixed, oth)
+    )(weights, oth, held, out)
 
 
 def swap(x):
@@ -296,8 +324,8 @@
     keep = stage(third_kernel, "third", pltpu.VMEM((128, HALF), F32), hidden, w_out)
     summed = (keep + swap(send).astype(F32)).astype(BF16).reshape(16, 1, 8, HALF)
     own = sum_parts(exchange(jnp.broadcast_to(summed, (16, 4, 8, HALF)).reshape(64, 8, HALF)))
-    mixed = stage(mix_own_kernel, "mix_own", pltpu.VMEM(weights.shape[:2] + (HALF,), BF16), weights, own)
-    return mix(weights, mixed, swap(own))
+    out, held = mix_own(weights, own)
+    return mix(weights, swap(own), held, out)
 
 
 def solution(mesh):

time: 63.4 us -> 63.4 us (level)
    pallas_call x1 -> x2, Pallas kernels: 2.41 us -> 3.27 us  [the longest x1 2.3 us: mix(): pl.pallas_call(functools.partial(mix_kernel, pieces, EARLY), out_shape=ja...]
    pallas_call x4 -> x3, Pallas kernels: 3.56 us -> 2.75 us  [stage(): pl.pallas_call(kernel, out_shape=outs, compiler_params=pltpu.CompilerPara...]
  transfers between devices with their start and end apart: 4 -> 4, of which waited for: 4 -> 3; matrix products, arithmetic and copies ran while one was open for 0% -> 0% of each run, Pallas kernels for 5% -> 5%
where the time goes in v5:
time: 63.4 us; the launch traced here: 63.3 us
  blocking collectives  44.5 us (70%)
  Pallas kernels  11.8 us (19%)
  starting transfers between devices  5.88 us (9%)
  waiting for transfers between devices  0.88 us (1%)
    all_to_all x2, blocking collectives, exchange(): return lax.all_to_all(x, ('dp', 'x'), 0, 0, tiled=True)  44.5 us
    ppermute x4, starting transfers between devices, swap(): return lax.ppermute(x, 'core', [(0, 1), (1, 0)])  5.88 us
    pallas_call x1, Pallas kernels, gather(): pl.pallas_call(functools.partial(gather_kernel, pieces), out_shape=[pltpu...  3.99 us
    pallas_call x3, Pallas kernels, stage(): pl.pallas_call(kernel, out_shape=outs, compiler_params=pltpu.CompilerPara...  2.75 us
    pallas_call x1, Pallas kernels, mix(): pl.pallas_call(functools.partial(mix_kernel, pieces, EARLY), out_shape=ja...  2.3 us
  transfers between devices with their start and end apart: 4, of which 3 were waited for; matrix products, arithmetic and copies ran while one was open for 0% of the time, Pallas kernels for 5%

profile of v5, /device:TPU:1, one launch (start us, length us, event | category | flops | bytes accessed | tf_op | source)
XLA Modules:
  0.0 63.3 jit_solution(16616334767418509285)
XLA Ops:
  0.0 4.0 %gather.1 = (bf16[2,64,768]{2,1,0:T(8,128)(2,1)S(1)}, f32[2,64,128]{2,1,0:T(8,128)S(1)}, bf16[2,64,1024]{2,1,0:T(8,128)(2,1)S(1)}, f32[2,64,1024]{2,1,0:T(8,128)S(1)}, bf16[2,1024,1280]{2,1,0:T(8,128)(2,1)S(1)}) custom-call(bf16[2,1024,1280]{2,1,0:T(8,128)(2,1)} %tokens_hbm.1, bf16[64,1280]{1,0:T(8,128)(2,1)} %bitcast.9), custom_call_target="tpu_custom_call" | custom-call | flops 503316480 | bytes 5242880 | tf_op jit(solution)/shard_map/gather/pallas_call | solution.py:71
  4.0 1.5 %collective-permute-start = (bf16[2,64,768]{2,1,0:T(8,128)(2,1)S(1)}, bf16[2,64,768]{2,1,0:T(8,128)(2,1)S(1)}, u32[]{:S(2)}, u32[]{:S(2)}) collective-permute-start(bf16[2,64,768]{2,1,0:T(8,128)(2,1)S(1)} %get-tuple-element.22), channel_id=1, source_target_pairs={{0,1},{1,0},{2,3},{3,2},{4,5},{5,4},{6,7},{7,6},{8,9},{9,8},{10,11... | collective-permute-start | bytes 589832 | tf_op jit(solution)/shard_map/ppermute | solution.py:307
  5.5 0.3 combine.1.combine_ref
  5.8 0.0 slice-start
  5.8 0.6 keep_half.1.keep_ref
  6.4 0.2 collective-permute-done.recv_ref
  6.6 0.0 slice-start.2
  6.6 0.0 slice-start.1
  6.6 0.0 slice-start.3
  6.6 0.3 pack.1
  6.9 26.5 %all_to_all.10.parts_ref = bf16[64,8,768]{2,1,0:T(8,128)(2,1)S(1)} all-to-all(bf16[64,8,768]{2,1,0:T(8,128)(2,1)S(1)} %pack.1), channel_id=1, replica_groups=mesh['dp'=16,'x'=4,'core'=2] {'dp','x'}, dimensions={0} | all-to-all | bytes 1572864 | tf_op jit(solution)/shard_map/all_to_all | solution.py:311
  33.4 0.3 reduce.1.own_ref
  33.8 2.0 %collective-permute-start.1 = (bf16[128,640]{1,0:T(8,128)(2,1)S(1)}, bf16[128,640]{1,0:T(8,128)(2,1)S(1)}, u32[]{:S(2)}, u32[]{:S(2)}) collective-permute-start(bf16[128,640]{1,0:T(8,128)(2,1)S(1)} %reduce.1.own_ref), channel_id=1, source_target_pairs={{0,1},{1,0},{2,3},{3,2},{4,5},{5,4},{6,7},{7,6},{8,9},{9,8},{10,11... | collective-permute-start | bytes 491528 | tf_op jit(solution)/shard_map/ppermute | solution.py:307
  35.7 0.0 slice-done
  35.7 0.0 slice-done.1
  35.7 0.7 %first.1.pre_ref = f32[128,640]{1,0:T(8,128)S(1)} custom-call(bf16[128,640]{1,0:T(8,128)(2,1)S(1)} %reduce.1.own_ref, bf16[4,1280,640]{2,1,0:T(8,128)(2,1)S(1)} %bitcast.5), custom_call_target="tpu_custom_call" | custom-call | flops 429916160 | bytes 6717440 | tf_op jit(solution)/shard_map/first/pallas_call | solution.py:191
  36.4 0.3 collective-permute-done.1.oth_ref
  36.8 0.0 slice-done.2
  36.8 0.0 slice-done.3
  36.8 1.4 %second.1 = (bf16[128,640]{1,0:T(8,128)(2,1)S(1)}, bf16[128,640]{1,0:T(8,128)(2,1)S(1)}) custom-call(f32[128,640]{1,0:T(8,128)S(1)} %first.1.pre_ref, bf16[128,640]{1,0:T(8,128)(2,1)S(1)} %collective-permute-done.1.oth_ref, bf16[4,1280,640]{2,1,0:T(8,128)(2,1)S(1)} %bitcast.5, bf16[4,640,1280]{2,1,0:T(8,128)(2,1)S(1)} %bitcast.7), custom_call_target="tpu_custom_call" | custom-call | flops 859832320 | bytes 13434880 | tf_op jit(solution)/shard_map/second/pallas_call | solution.py:191
  38.2 0.5 collective-permute-start.2
  38.6 0.7 %third.1 = f32[128,640]{1,0:T(8,128)S(1)} custom-call(bf16[128,640]{1,0:T(8,128)(2,1)S(1)} %get-tuple-element.23.hidden_ref, bf16[4,640,1280]{2,1,0:T(8,128)(2,1)S(1)} %bitcast.7), custom_call_target="tpu_custom_call" | custom-call | flops 429916160 | bytes 6717440 | tf_op jit(solution)/shard_map/third/pallas_call | solution.py:191
  39.3 0.3 collective-permute-done.2
  39.7 0.1 broadcast_in_dim.8
  39.8 18.0 %all_to_all.11.parts_ref = bf16[64,8,640]{2,1,0:T(8,128)(2,1)S(1)} all-to-all(bf16[64,8,640]{2,1,0:T(8,128)(2,1)S(1)} %bitcast.8), channel_id=1, replica_groups=mesh['dp'=16,'x'=4,'core'=2] {'dp','x'}, dimensions={0} | all-to-all | bytes 1310720 | tf_op jit(solution)/shard_map/all_to_all | solution.py:311
  57.7 0.3 sum_parts.1.own_ref
  58.0 1.9 %collective-permute-start.3 = (bf16[2,64,640]{2,1,0:T(8,128)(2,1)S(1)}, bf16[2,64,640]{2,1,0:T(8,128)(2,1)S(1)}, u32[]{:S(2)}, u32[]{:S(2)}) collective-permute-start(bf16[2,64,640]{2,1,0:T(8,128)(2,1)S(1)} %sum_parts.1.own_ref), channel_id=1, source_target_pairs={{0,1},{1,0},{2,3},{3,2},{4,5},{5,4},{6,7},{7,6},{8,9},{9,8},{10,11... | collective-permute-start | bytes 491528 | tf_op jit(solution)/shard_map/ppermute | solution.py:307
  59.9 1.0 %mix_own.1 = (bf16[2,1024,1280]{2,1,0:T(8,128)(2,1)}, bf16[2,1024,640]{2,1,0:T(8,128)(2,1)S(1)}) custom-call(bf16[2,1024,64]{2,1,0:T(8,128)(2,1)S(1)} %combine.1.combine_ref, bf16[2,64,640]{2,1,0:T(8,128)(2,1)S(1)} %sum_parts.1.own_ref), custom_call_target="tpu_custom_call" | custom-call | flops 167772160 | bytes 2621440 | tf_op jit(solution)/shard_map/mix_own/pallas_call | solution.py:255
  60.9 0.0 collective-permute-done.3.oth_ref
  61.0 2.3 %mix.1 = bf16[2,1024,1280]{2,1,0:T(8,128)(2,1)} custom-call(bf16[2,1024,64]{2,1,0:T(8,128)(2,1)S(1)} %combine.1.combine_ref, bf16[2,64,640]{2,1,0:T(8,128)(2,1)S(1)} %collective-permute-done.3.oth_ref, bf16[2,1024,640]{2,1,0:T(8,128)(2,1)S(1)} %get-tuple-element.25.held_ref, bf16[2,1024,1280]{2,1,0:T(8,128)(2,1)} %get-tuple-element.26._), custom_call_target="tpu_custom_call", output_to_operand_aliasing={{}: (3, {})} | custom-call | tf_op jit(solution)/shard_map/mix/pallas_call | solution.py:294
  (3 shorter events, 0.0 us)
Async XLA Ops:
  4.0 2.6 %collective-permute-start = (bf16[2,64,768]{2,1,0:T(8,128)(2,1)S(1)}, bf16[2,64,768]{2,1,0:T(8,128)(2,1)S(1)}, u32[]{:S(2)}, u32[]{:S(2)}) collective-permute-start(bf16[2,64,768]{2,1,0:T(8,128)(2,1)S(1)} %get-tuple-element.22), channel_id=1, source_target_pairs={{0,1},{1,0},{2,3},{3,2},{4,5},{5,4},{6,7},{7,6},{8,9},{9,8},{10,11... | collective-permute-start | bytes 589832 | tf_op jit(solution)/shard_map/ppermute | solution.py:307
  5.8 30.0 %slice-start = ((s8[6553600]{0:T(1024)(128)(4,1)}), s8[4194304]{0:T(1024)(128)(4,1)S(1)}, s32[]{:S(2)}) async-start(s8[6553600]{0:T(1024)(128)(4,1)} %bitcast.4), calls=%async_computation.2 | async-start | bytes 8388608
  6.6 30.2 %slice-start.2 = ((s8[6553600]{0:T(1024)(128)(4,1)}), s8[4194304]{0:T(1024)(128)(4,1)S(1)}, s32[]{:S(2)}) async-start(s8[6553600]{0:T(1024)(128)(4,1)} %bitcast.6), calls=%async_computation.4 | async-start | bytes 8388608
  6.6 29.2 %slice-start.1 = ((s8[6553600]{0:T(1024)(128)(4,1)}), s8[2359296]{0:T(1024)(128)(4,1)S(1)}, s32[]{:S(2)}) async-start(s8[6553600]{0:T(1024)(128)(4,1)} %bitcast.4), calls=%async_computation.3 | async-start | bytes 4718592
  6.6 30.2 %slice-start.3 = ((s8[6553600]{0:T(1024)(128)(4,1)}), s8[2359296]{0:T(1024)(128)(4,1)S(1)}, s32[]{:S(2)}) async-start(s8[6553600]{0:T(1024)(128)(4,1)} %bitcast.6), calls=%async_computation.5 | async-start | bytes 4718592
  33.8 3.0 %collective-permute-start.1 = (bf16[128,640]{1,0:T(8,128)(2,1)S(1)}, bf16[128,640]{1,0:T(8,128)(2,1)S(1)}, u32[]{:S(2)}, u32[]{:S(2)}) collective-permute-start(bf16[128,640]{1,0:T(8,128)(2,1)S(1)} %reduce.1.own_ref), channel_id=1, source_target_pairs={{0,1},{1,0},{2,3},{3,2},{4,5},{5,4},{6,7},{7,6},{8,9},{9,8},{10,11... | collective-permute-start | bytes 491528 | tf_op jit(solution)/shard_map/ppermute | solution.py:307
  38.2 1.5 %collective-permute-start.2 = (bf16[128,640]{1,0:T(8,128)(2,1)S(1)}, bf16[128,640]{1,0:T(8,128)(2,1)S(1)}, u32[]{:S(2)}, u32[]{:S(2)}) collective-permute-start(bf16[128,640]{1,0:T(8,128)(2,1)S(1)} %get-tuple-element.24), channel_id=1, source_target_pairs={{0,1},{1,0},{2,3},{3,2},{4,5},{5,4},{6,7},{7,6},{8,9},{9,8},{10,11... | collective-permute-start | bytes 491528 | tf_op jit(solution)/shard_map/ppermute | solution.py:307
  58.0 3.0 %collective-permute-start.3 = (bf16[2,64,640]{2,1,0:T(8,128)(2,1)S(1)}, bf16[2,64,640]{2,1,0:T(8,128)(2,1)S(1)}, u32[]{:S(2)}, u32[]{:S(2)}) collective-permute-start(bf16[2,64,640]{2,1,0:T(8,128)(2,1)S(1)} %sum_parts.1.own_ref), channel_id=1, source_target_pairs={{0,1},{1,0},{2,3},{3,2},{4,5},{5,4},{6,7},{7,6},{8,9},{9,8},{10,11... | collective-permute-start | bytes 491528 | tf_op jit(solution)/shard_map/ppermute | solution.py:307

commit v6 on v5

--- a/solution.py
+++ b/solution.py
@@ -223,7 +223,8 @@
     part = lax.broadcasted_iota(jnp.int32, (128, 512), 1)
     same = ((row // 64) * 4 + row % 4 == part % 8) & ((row % 64) // 4 == part // 32)
     ones = jnp.where(same, 1.0, 0.0).astype(BF16)
-    total = jnp.dot(ones, parts_ref[...].reshape(512, HALF), preferred_element_type=F32)
+    parts = parts_ref[...].astype(F32).reshape(512, HALF).astype(BF16)
+    total = jnp.dot(ones, parts, preferred_element_type=F32)
     out_ref[...] = total.astype(BF16).reshape(2, 64, HALF)
 
 

time: 63.4 us -> 63.4 us (level)
  no operation moved by 1% of the time
where the time goes in v6:
time: 63.4 us; the launch traced here: 63.3 us
  blocking collectives  44.5 us (70%)
  Pallas kernels  11.8 us (19%)
  starting transfers between devices  5.88 us (9%)
  waiting for transfers between devices  0.88 us (1%)
    all_to_all x2, blocking collectives, exchange(): return lax.all_to_all(x, ('dp', 'x'), 0, 0, tiled=True)  44.5 us
    ppermute x4, starting transfers between devices, swap(): return lax.ppermute(x, 'core', [(0, 1), (1, 0)])  5.88 us
    pallas_call x1, Pallas kernels, gather(): pl.pallas_call(functools.partial(gather_kernel, pieces), out_shape=[pltpu...  3.99 us
    pallas_call x3, Pallas kernels, stage(): pl.pallas_call(kernel, out_shape=outs, compiler_params=pltpu.CompilerPara...  2.75 us
    pallas_call x1, Pallas kernels, mix(): pl.pallas_call(functools.partial(mix_kernel, pieces, EARLY), out_shape=ja...  2.3 us
  transfers between devices with their start and end apart: 4, of which 3 were waited for; matrix products, arithmetic and copies ran while one was open for 0% of the time, Pallas kernels for 5%

profile of v6, /device:TPU:1, one launch (start us, length us, event | category | flops | bytes accessed | tf_op | source)
XLA Modules:
  0.0 63.3 jit_solution(16616334767418509285)
XLA Ops:
  0.0 4.0 %gather.1 = (bf16[2,64,768]{2,1,0:T(8,128)(2,1)S(1)}, f32[2,64,128]{2,1,0:T(8,128)S(1)}, bf16[2,64,1024]{2,1,0:T(8,128)(2,1)S(1)}, f32[2,64,1024]{2,1,0:T(8,128)S(1)}, bf16[2,1024,1280]{2,1,0:T(8,128)(2,1)S(1)}) custom-call(bf16[2,1024,1280]{2,1,0:T(8,128)(2,1)} %tokens_hbm.1, bf16[64,1280]{1,0:T(8,128)(2,1)} %bitcast.9), custom_call_target="tpu_custom_call" | custom-call | flops 503316480 | bytes 5242880 | tf_op jit(solution)/shard_map/gather/pallas_call | solution.py:71
  4.0 1.5 %collective-permute-start = (bf16[2,64,768]{2,1,0:T(8,128)(2,1)S(1)}, bf16[2,64,768]{2,1,0:T(8,128)(2,1)S(1)}, u32[]{:S(2)}, u32[]{:S(2)}) collective-permute-start(bf16[2,64,768]{2,1,0:T(8,128)(2,1)S(1)} %get-tuple-element.22), channel_id=1, source_target_pairs={{0,1},{1,0},{2,3},{3,2},{4,5},{5,4},{6,7},{7,6},{8,9},{9,8},{10,11... | collective-permute-start | bytes 589832 | tf_op jit(solution)/shard_map/ppermute | solution.py:308
  5.5 0.3 combine.1.combine_ref
  5.8 0.0 slice-start
  5.8 0.6 keep_half.1.keep_ref
  6.4 0.2 collective-permute-done.recv_ref
  6.6 0.0 slice-start.2
  6.6 0.0 slice-start.1
  6.6 0.0 slice-start.3
  6.6 0.3 pack.1
  6.9 26.5 %all_to_all.10.parts_ref = bf16[64,8,768]{2,1,0:T(8,128)(2,1)S(1)} all-to-all(bf16[64,8,768]{2,1,0:T(8,128)(2,1)S(1)} %pack.1), channel_id=1, replica_groups=mesh['dp'=16,'x'=4,'core'=2] {'dp','x'}, dimensions={0} | all-to-all | bytes 1572864 | tf_op jit(solution)/shard_map/all_to_all | solution.py:312
  33.4 0.3 reduce.1.own_ref
  33.8 2.0 %collective-permute-start.1 = (bf16[128,640]{1,0:T(8,128)(2,1)S(1)}, bf16[128,640]{1,0:T(8,128)(2,1)S(1)}, u32[]{:S(2)}, u32[]{:S(2)}) collective-permute-start(bf16[128,640]{1,0:T(8,128)(2,1)S(1)} %reduce.1.own_ref), channel_id=1, source_target_pairs={{0,1},{1,0},{2,3},{3,2},{4,5},{5,4},{6,7},{7,6},{8,9},{9,8},{10,11... | collective-permute-start | bytes 491528 | tf_op jit(solution)/shard_map/ppermute | solution.py:308
  35.7 0.0 slice-done
  35.7 0.0 slice-done.1
  35.7 0.7 %first.1.pre_ref = f32[128,640]{1,0:T(8,128)S(1)} custom-call(bf16[128,640]{1,0:T(8,128)(2,1)S(1)} %reduce.1.own_ref, bf16[4,1280,640]{2,1,0:T(8,128)(2,1)S(1)} %bitcast.5), custom_call_target="tpu_custom_call" | custom-call | flops 429916160 | bytes 6717440 | tf_op jit(solution)/shard_map/first/pallas_call | solution.py:191
  36.4 0.3 collective-permute-done.1.oth_ref
  36.8 0.0 slice-done.2
  36.8 0.0 slice-done.3
  36.8 1.4 %second.1 = (bf16[128,640]{1,0:T(8,128)(2,1)S(1)}, bf16[128,640]{1,0:T(8,128)(2,1)S(1)}) custom-call(f32[128,640]{1,0:T(8,128)S(1)} %first.1.pre_ref, bf16[128,640]{1,0:T(8,128)(2,1)S(1)} %collective-permute-done.1.oth_ref, bf16[4,1280,640]{2,1,0:T(8,128)(2,1)S(1)} %bitcast.5, bf16[4,640,1280]{2,1,0:T(8,128)(2,1)S(1)} %bitcast.7), custom_call_target="tpu_custom_call" | custom-call | flops 859832320 | bytes 13434880 | tf_op jit(solution)/shard_map/second/pallas_call | solution.py:191
  38.2 0.5 collective-permute-start.2
  38.6 0.7 %third.1 = f32[128,640]{1,0:T(8,128)S(1)} custom-call(bf16[128,640]{1,0:T(8,128)(2,1)S(1)} %get-tuple-element.23.hidden_ref, bf16[4,640,1280]{2,1,0:T(8,128)(2,1)S(1)} %bitcast.7), custom_call_target="tpu_custom_call" | custom-call | flops 429916160 | bytes 6717440 | tf_op jit(solution)/shard_map/third/pallas_call | solution.py:191
  39.3 0.3 collective-permute-done.2
  39.7 0.1 broadcast_in_dim.8
  39.8 18.0 %all_to_all.11.parts_ref = bf16[64,8,640]{2,1,0:T(8,128)(2,1)S(1)} all-to-all(bf16[64,8,640]{2,1,0:T(8,128)(2,1)S(1)} %bitcast.8), channel_id=1, replica_groups=mesh['dp'=16,'x'=4,'core'=2] {'dp','x'}, dimensions={0} | all-to-all | bytes 1310720 | tf_op jit(solution)/shard_map/all_to_all | solution.py:312
  57.7 0.3 sum_parts.1.own_ref
  58.0 1.9 %collective-permute-start.3 = (bf16[2,64,640]{2,1,0:T(8,128)(2,1)S(1)}, bf16[2,64,640]{2,1,0:T(8,128)(2,1)S(1)}, u32[]{:S(2)}, u32[]{:S(2)}) collective-permute-start(bf16[2,64,640]{2,1,0:T(8,128)(2,1)S(1)} %sum_parts.1.own_ref), channel_id=1, source_target_pairs={{0,1},{1,0},{2,3},{3,2},{4,5},{5,4},{6,7},{7,6},{8,9},{9,8},{10,11... | collective-permute-start | bytes 491528 | tf_op jit(solution)/shard_map/ppermute | solution.py:308
  59.9 1.0 %mix_own.1 = (bf16[2,1024,1280]{2,1,0:T(8,128)(2,1)}, bf16[2,1024,640]{2,1,0:T(8,128)(2,1)S(1)}) custom-call(bf16[2,1024,64]{2,1,0:T(8,128)(2,1)S(1)} %combine.1.combine_ref, bf16[2,64,640]{2,1,0:T(8,128)(2,1)S(1)} %sum_parts.1.own_ref), custom_call_target="tpu_custom_call" | custom-call | flops 167772160 | bytes 2621440 | tf_op jit(solution)/shard_map/mix_own/pallas_call | solution.py:256
  60.9 0.0 collective-permute-done.3.oth_ref
  61.0 2.3 %mix.1 = bf16[2,1024,1280]{2,1,0:T(8,128)(2,1)} custom-call(bf16[2,1024,64]{2,1,0:T(8,128)(2,1)S(1)} %combine.1.combine_ref, bf16[2,64,640]{2,1,0:T(8,128)(2,1)S(1)} %collective-permute-done.3.oth_ref, bf16[2,1024,640]{2,1,0:T(8,128)(2,1)S(1)} %get-tuple-element.25.held_ref, bf16[2,1024,1280]{2,1,0:T(8,128)(2,1)} %get-tuple-element.26._), custom_call_target="tpu_custom_call", output_to_operand_aliasing={{}: (3, {})} | custom-call | tf_op jit(solution)/shard_map/mix/pallas_call | solution.py:295
  (3 shorter events, 0.0 us)
Async XLA Ops:
  4.0 2.6 %collective-permute-start = (bf16[2,64,768]{2,1,0:T(8,128)(2,1)S(1)}, bf16[2,64,768]{2,1,0:T(8,128)(2,1)S(1)}, u32[]{:S(2)}, u32[]{:S(2)}) collective-permute-start(bf16[2,64,768]{2,1,0:T(8,128)(2,1)S(1)} %get-tuple-element.22), channel_id=1, source_target_pairs={{0,1},{1,0},{2,3},{3,2},{4,5},{5,4},{6,7},{7,6},{8,9},{9,8},{10,11... | collective-permute-start | bytes 589832 | tf_op jit(solution)/shard_map/ppermute | solution.py:308
  5.8 30.0 %slice-start = ((s8[6553600]{0:T(1024)(128)(4,1)}), s8[4194304]{0:T(1024)(128)(4,1)S(1)}, s32[]{:S(2)}) async-start(s8[6553600]{0:T(1024)(128)(4,1)} %bitcast.4), calls=%async_computation.2 | async-start | bytes 8388608
  6.6 30.2 %slice-start.2 = ((s8[6553600]{0:T(1024)(128)(4,1)}), s8[4194304]{0:T(1024)(128)(4,1)S(1)}, s32[]{:S(2)}) async-start(s8[6553600]{0:T(1024)(128)(4,1)} %bitcast.6), calls=%async_computation.4 | async-start | bytes 8388608
  6.6 29.2 %slice-start.1 = ((s8[6553600]{0:T(1024)(128)(4,1)}), s8[2359296]{0:T(1024)(128)(4,1)S(1)}, s32[]{:S(2)}) async-start(s8[6553600]{0:T(1024)(128)(4,1)} %bitcast.4), calls=%async_computation.3 | async-start | bytes 4718592
  6.6 30.2 %slice-start.3 = ((s8[6553600]{0:T(1024)(128)(4,1)}), s8[2359296]{0:T(1024)(128)(4,1)S(1)}, s32[]{:S(2)}) async-start(s8[6553600]{0:T(1024)(128)(4,1)} %bitcast.6), calls=%async_computation.5 | async-start | bytes 4718592
  33.8 3.0 %collective-permute-start.1 = (bf16[128,640]{1,0:T(8,128)(2,1)S(1)}, bf16[128,640]{1,0:T(8,128)(2,1)S(1)}, u32[]{:S(2)}, u32[]{:S(2)}) collective-permute-start(bf16[128,640]{1,0:T(8,128)(2,1)S(1)} %reduce.1.own_ref), channel_id=1, source_target_pairs={{0,1},{1,0},{2,3},{3,2},{4,5},{5,4},{6,7},{7,6},{8,9},{9,8},{10,11... | collective-permute-start | bytes 491528 | tf_op jit(solution)/shard_map/ppermute | solution.py:308
  38.2 1.5 %collective-permute-start.2 = (bf16[128,640]{1,0:T(8,128)(2,1)S(1)}, bf16[128,640]{1,0:T(8,128)(2,1)S(1)}, u32[]{:S(2)}, u32[]{:S(2)}) collective-permute-start(bf16[128,640]{1,0:T(8,128)(2,1)S(1)} %get-tuple-element.24), channel_id=1, source_target_pairs={{0,1},{1,0},{2,3},{3,2},{4,5},{5,4},{6,7},{7,6},{8,9},{9,8},{10,11... | collective-permute-start | bytes 491528 | tf_op jit(solution)/shard_map/ppermute | solution.py:308
  58.0 3.0 %collective-permute-start.3 = (bf16[2,64,640]{2,1,0:T(8,128)(2,1)S(1)}, bf16[2,64,640]{2,1,0:T(8,128)(2,1)S(1)}, u32[]{:S(2)}, u32[]{:S(2)}) collective-permute-start(bf16[2,64,640]{2,1,0:T(8,128)(2,1)S(1)} %sum_parts.1.own_ref), channel_id=1, source_target_pairs={{0,1},{1,0},{2,3},{3,2},{4,5},{5,4},{6,7},{7,6},{8,9},{9,8},{10,11... | collective-permute-start | bytes 491528 | tf_op jit(solution)/shard_map/ppermute | solution.py:308
